TPU v7x, 32 devices: a whole 2x2x4 slice. The times are simulated.
32 devices in a mesh: rows: 16 (over z, y, core), cols: 2 (over x).
Axes of the slice: x: 2, y: 2, z: 4, core: 2. Of those that a mesh axis runs over, the one named last changes fastest.
Arguments:
- images: float32 [128, 32, 128], P('rows'), may hold values from -6 to 6
- gauge_pixel: int32 [32768], P('rows'), may hold values from 0 to 32767
- row_mask: int32 [32768], P('rows'), may hold values 0 or 1
- gauge_counts: int32 [16], P('rows'), may hold values from 1 to 2048, as said below
- targets: float32 [32768], P('rows'), may hold values from -10 to 10
- theta: float32 [64, 8], replicated, may hold values from -2.5 to 2.5
- amplitude: float32 [64], replicated, may hold values from 0.5 to 1.5
- damping: float32 [], replicated, may hold values from 0.05 to 0.3
Outputs:
- r_factor: float32 [512, 512], replicated
- new_theta: float32 [64, 8], replicated
- predicted: float32 [32768], P(('rows', 'cols'))
Inputs may be any that keep to these rules, and one draw needn't show every extreme that they name: The slots in use on an index of rows are its first gauge_counts slots; one index of rows uses all 2048.
All inputs are finite; a program needn't handle non-finite values. No bound on the sum of `row_mask` on one device may be relied on, other than what follows from the above.
Results may differ from a plain program's by a relative error of at most 0.0003.
Values sent between devices are 32-bit elements; how exact they have to be, the bound alone decides.
No kernel may reach another device: no remote copies, remote signals or barrier semaphores. Data moves between devices by JAX's collectives and lax.ppermute only.
A program may use at most 64 MiB of HBM per device.

v0:
```python
import functools
import math

import jax
import jax.numpy as jnp
from jax import lax
from jax.experimental import pallas as pl
from jax.experimental.pallas import tpu as pltpu
from jax.sharding import PartitionSpec as P

Y_ORDERS = [0, 1, 0, 2, 1, 0, 0, 0]
X_ORDERS = [0, 0, 1, 0, 1, 2, 0, 2]
SIGMAS = [1.5, 1.5, 1.5, 1.5, 1.5, 1.5, 3.0, 3.0]

F32 = jnp.float32
BF16 = jnp.bfloat16
NN = (((1,), (0,)), ((), ()))
NT = (((1,), (1,)), ((), ()))
VMEM = pl.BlockSpec(memory_space=pltpu.VMEM)
SMEM = pl.BlockSpec(memory_space=pltpu.SMEM)
PACK = 168
GROUP = 16
BLK = 64


def iota(shape, dim):
    return lax.broadcasted_iota(jnp.int32, shape, dim)


def kernel_scale(order, width):
    total = 0.0
    for t in range(-12, 13):
        e = math.exp(-t * t / (2.0 * width * width))
        if order == 1:
            e = -t / width**2 * e
        elif order == 2:
            e = (t * t / width**4 - 1.0 / width**2) * e
        total += e * e
    return 1.0 / math.sqrt(total)


def kernel_values(lag, order, width):
    e = jnp.exp(lag * lag * (-1.0 / (2.0 * width * width)))
    if order == 1:
        e = lag * (-1.0 / width**2) * e
    elif order == 2:
        e = (lag * lag * (1.0 / width**4) - 1.0 / width**2) * e
    return e * kernel_scale(order, width)


def split(a):
    hi = a.astype(BF16)
    return hi, (a - hi.astype(F32)).astype(BF16)


def dot(a, b, dims=NN):
    return lax.dot_general(a, b, dims, preferred_element_type=F32)


def dot3(a, b, dims=NN):
    ah, al = a if isinstance(a, tuple) else split(a)
    bh, bl = b if isinstance(b, tuple) else split(b)
    return dot(ah, bh, dims) + (dot(ah, bl, dims) + dot(al, bh, dims))


def dot_full(a, b, dims=NN):
    return lax.dot_general(
        a, b, dims, precision=lax.Precision.HIGHEST, preferred_element_type=F32
    )


def front(
    ncols,
    place_ref,
    count_ref,
    img_ref,
    pix_ref,
    mask_ref,
    target_ref,
    theta_ref,
    amp_ref,
    keep_ref,
    send_ref,
    slope_ref,
    phi_ref,
    resid_ref,
    feat_ref,
    jh_ref,
    jl_ref,
    all_phi_ref,
    all_sr_ref,
    all_slope_ref,
    all_resid_ref,
):
    half = place_ref[0]
    quarter = place_ref[1]
    column = place_ref[2]
    count = count_ref[0]
    slots = pix_ref.shape[1]
    rows, breadth = img_ref.shape
    height = 32
    chans, basis = theta_ref.shape

    image_t = split(img_ref[...].T)
    lefts = {}
    for order, width in sorted(set(zip(Y_ORDERS, SIGMAS))):
        lag = ((iota((height, breadth), 1) & (height - 1)) - iota((height, breadth), 0)).astype(F32)
        table = kernel_values(lag, order, width)
        wide = jnp.concatenate([table] * (rows // height), 0)
        wide = jnp.concatenate([wide] * (rows // breadth), 1)
        same = (iota((rows, rows), 0) // height) == (iota((rows, rows), 1) // height)
        lefts[order, width] = split(dot3(image_t, jnp.where(same, wide, 0.0)))
    lag = (iota((breadth, breadth), 0) - iota((breadth, breadth), 1)).astype(F32)
    for k in range(basis):
        right = kernel_values(lag, X_ORDERS[k], SIGMAS[k])
        hi, lo = split(dot3(right, lefts[Y_ORDERS[k], SIGMAS[k]]))
        feat_ref[k] = jnp.concatenate([hi, lo], 1)

    theta = theta_ref[...]
    diag = iota((chans, chans), 0) == iota((chans, chans), 1)
    amp = jnp.sum(jnp.where(diag, amp_ref[...], 0.0), axis=1, keepdims=True)

    chunk = min(512, slots)
    live_total = jnp.zeros((1, 1), F32)
    for start in range(0, slots, chunk):
        at = slice(start, start + chunk)
        pix = pix_ref[:, at]
        row = pix // breadth
        col = pix & (breadth - 1)
        pick_row = jnp.where(iota((rows, chunk), 0) == row, 1.0, 0.0).astype(BF16)
        pick_row = jnp.concatenate([pick_row, pick_row], 0)
        pick_col = iota((breadth, chunk), 0) == col
        phis = []
        for k in range(basis):
            found = dot(feat_ref[k], pick_row)
            phis.append(jnp.sum(jnp.where(pick_col, found, 0.0), axis=0, keepdims=True))
        phi = jnp.concatenate(phis, 0)
        all_phi_ref[:, at] = phi
        slot = iota((1, chunk), 1) + start
        live = jnp.where((slot < count) & (mask_ref[:, at] == 1), 1.0, 0.0)
        live_total = live_total + jnp.sum(live, axis=1, keepdims=True)
        z = theta[:, 0:1] * phis[0]
        for k in range(1, basis):
            z = z + theta[:, k : k + 1] * phis[k]
        act = jnp.tanh(z)
        model = jnp.sum(amp * act, axis=0, keepdims=True)
        resid = live * (model - target_ref[:, at])
        slope = (live * amp) * (1.0 - act * act)
        all_resid_ref[:, at] = resid
        all_slope_ref[:, at] = slope
        all_sr_ref[:, at] = slope * resid
        for k in range(basis):
            hi, lo = split(slope * phis[k])
            place = pl.multiple_of(((k + 4 * half) % basis) * chans, chans)
            jh_ref[pl.ds(place, chans), at] = hi
            jl_ref[pl.ds(place, chans), at] = lo

    own = slots // ncols
    mine = pl.ds(pl.multiple_of(column * own, own), own)
    slope_ref[...] = all_slope_ref[:, mine]
    phi_ref[...] = all_phi_ref[:, mine]
    resid_ref[...] = all_resid_ref[:, mine]

    grad = dot3(all_phi_ref[...], all_sr_ref[...], NT)

    packs = []
    for part in range(2):
        lo_row = 2 * part * chans
        a = slice(lo_row, lo_row + 2 * chans)
        b = slice(lo_row, lo_row + 6 * chans)
        blocks = dot3((jh_ref[a], jl_ref[a]), (jh_ref[b], jl_ref[b]), NT)
        first = blocks[:chans, : 5 * chans]
        second = blocks[chans:, chans:]
        r = iota((chans, 5 * chans), 0)
        c = iota((chans, 5 * chans), 1) & (chans - 1)
        fold = jnp.where(r >= c, first, second)
        lost = jnp.sum(jnp.where(r == c, second, 0.0), axis=0, keepdims=True)
        last = fold[:, 4 * chans :]
        extra = [lost[:, d * chans : (d + 1) * chans] for d in range(5)]
        extra.append(jnp.broadcast_to(live_total, (1, chans)))
        extra.append(jnp.zeros((2, chans), F32))
        tail = jnp.concatenate([grad, jnp.concatenate(extra, 0)], 1)
        packs.append(
            (
                fold[:, : 2 * chans],
                fold[:, 2 * chans : 4 * chans],
                jnp.concatenate([last[: chans // 2], last[chans // 2 :]], 1),
                tail,
            )
        )
    at = 0
    for one, two in zip(*packs):
        piece = pl.ds(at, one.shape[0])
        keep_ref[piece, :] = jnp.where(quarter == 0, one, two)
        send_ref[piece, :] = jnp.where(quarter == 0, two, one)
        at += one.shape[0]


def factor_block(work):
    tiles = [work[8 * t : 8 * t + 8] for t in range(BLK // 8)]
    sub = iota((8, 128), 0)

    def spread(x):
        return jnp.broadcast_to(x, (8, 128))

    for base in range(0, BLK, GROUP):
        t0 = base // 8
        left = range(t0, BLK // 8)
        cols = [
            {t: spread(tiles[t][:, base + m : base + m + 1]) for t in left} for m in range(GROUP)
        ]
        for m in range(GROUP):
            tp, s = (base + m) // 8, m % 8
            inverse = 1.0 / spread(cols[m][tp][s : s + 1])
            here = range(tp, BLK // 8)
            mult = {t: cols[m][t] * inverse for t in here}
            mult[tp] = jnp.where(sub > s, mult[tp], 0.0)
            for n in range(m + 1, GROUP):
                pivot_n = spread(cols[n][tp][s : s + 1])
                for t in here:
                    cols[n][t] = cols[n][t] - mult[t] * pivot_n
            pivot_row = spread(tiles[tp][s : s + 1])
            for t in here:
                tiles[t] = tiles[t] - mult[t] * pivot_row
    return jnp.concatenate(tiles, 0)


def back(
    place_ref,
    damping_ref,
    q0_ref,
    q1_ref,
    q2_ref,
    q3_ref,
    slope_ref,
    phi_ref,
    resid_ref,
    theta_ref,
    r_ref,
    new_theta_ref,
    pred_ref,
    pack_ref,
    plain_ref,
    mixed_ref,
    n_ref,
    inv_ref,
    x_ref,
):
    half = place_ref[0]
    quarter = place_ref[1]
    chans, basis = theta_ref.shape
    params = chans * basis
    pack_ref[2 * half + quarter] = q0_ref[...]
    pack_ref[2 * (1 - half) + quarter] = q1_ref[...]
    pack_ref[2 * half + (1 - quarter)] = q2_ref[...]
    pack_ref[2 * (1 - half) + (1 - quarter)] = q3_ref[...]

    total = pack_ref[0, PACK - 3 : PACK - 2, chans : chans + 1]
    scale = 1.0 / total
    r = iota((chans, chans), 0)
    c = iota((chans, chans), 1)

    def put(k, l, block):
        plain_ref[k * chans : (k + 1) * chans, l * chans : (l + 1) * chans] = block

    for q in range(4):
        tail = pack_ref[q, PACK - 8 :, chans:]
        folds = []
        for pair in range(2):
            f = pack_ref[q, pair * chans : (pair + 1) * chans, :]
            ft = f.T
            for d in range(2):
                folds.append((f[:, d * chans : (d + 1) * chans], ft[d * chans : (d + 1) * chans]))
        last = pack_ref[q, 2 * chans : 2 * chans + chans // 2, :]
        f = jnp.concatenate([last[:, :chans], last[:, chans:]], 0)
        folds.append((f, f.T))
        for d, (f, ft) in enumerate(folds):
            first = jnp.where(r >= c, f, ft)
            second = jnp.where(r < c, f, ft)
            second = jnp.where(r == c, tail[d : d + 1], second)
            k = 2 * q
            for k, block in ((2 * q, first), (2 * q + 1, second)):
                l = (k + d) % basis
                put(k, l, block)
                if d not in (0, 4):
                    put(l, k, block)
    tiles = params // 128
    per = 128 // chans
    for k in range(basis):
        for b in range(tiles):
            mixed_ref[b, pl.ds(k, chans, stride=basis), :] = plain_ref[
                k * chans : (k + 1) * chans, b * 128 : (b + 1) * 128
            ]
    for a in range(tiles):
        for b in range(tiles):
            t = mixed_ref[b, a * 128 : (a + 1) * 128, :].T * scale
            for e in range(per):
                n_ref[a, pl.ds(b * per + e, chans, stride=basis), :] = t[
                    e * chans : (e + 1) * chans
                ]
    grad = (pack_ref[0, PACK - 8 :, :] * scale).T[:chans]
    for k in range(basis):
        n_ref[tiles, pl.ds(k, chans, stride=basis), :] = jnp.broadcast_to(
            grad[:, k : k + 1], (chans, 128)
        )

    def load(at, first):
        return jnp.concatenate([n_ref[t, at, :] for t in range(first, tiles + 1)], 1)

    damping = damping_ref[0, 0]
    eye = iota((BLK, BLK), 0) == iota((BLK, BLK), 1)
    upper = iota((BLK, BLK), 0) <= iota((BLK, BLK), 1)
    blocks = params // BLK
    for j in range(blocks):
        at = slice(j * BLK, (j + 1) * BLK)
        first, skip = divmod(j * BLK, 128)
        a = n_ref[first, at, skip : skip + BLK] + jnp.where(eye, damping, 0.0)
        work = factor_block(jnp.concatenate([a, jnp.where(eye, 1.0, 0.0)], 1))
        pivots = jnp.sum(jnp.where(eye, work[:, :BLK], 0.0), axis=1, keepdims=True)
        work = work * lax.rsqrt(pivots)
        inverse = work[:, BLK:]
        inv_ref[j] = inverse
        panel = dot_full(inverse, load(at, first))
        x_ref[at, :] = panel[:, -128:]
        if first:
            r_ref[at, : first * 128] = jnp.zeros((BLK, first * 128), F32)
        r_ref[at, first * 128 :] = panel[:, :-128]
        r_ref[at, at] = jnp.where(upper, work[:, :BLK], 0.0)
        if skip:
            r_ref[at, first * 128 : j * BLK] = jnp.zeros((BLK, skip), F32)
        if j + 1 < blocks:
            nxt = (j + 1) * BLK // 128
            rest = panel[:, (nxt - first) * 128 :]
            update = dot_full(rest[:, :-128].T, rest)
            for t in range(nxt, tiles + 1):
                n_ref[t, nxt * 128 :, :] = (
                    n_ref[t, nxt * 128 :, :] - update[:, (t - nxt) * 128 : (t - nxt + 1) * 128]
                )

    for j in reversed(range(blocks)):
        at = slice(j * BLK, (j + 1) * BLK)
        y = x_ref[at, :]
        if j + 1 < blocks:
            y = y - dot_full(r_ref[at, (j + 1) * BLK :], x_ref[(j + 1) * BLK :, :])
        x_ref[at, :] = dot_full(inv_ref[j].T, y)

    lane = iota((chans, 128), 1)
    weight = jnp.zeros(slope_ref.shape, F32)
    move = jnp.zeros((chans, 128), F32)
    width = slope_ref.shape[1]
    for k in range(basis):
        step = -x_ref[pl.ds(k, chans, stride=basis), :]
        move = jnp.where(lane == k, step, move)
        wide = jnp.concatenate([step] * (width // 128), 1)
        weight = weight + wide * phi_ref[k : k + 1, :]
    new_theta_ref[...] = theta_ref[...] + move[:, :basis]
    pred_ref[...] = resid_ref[...] + jnp.sum(slope_ref[...] * weight, axis=0, keepdims=True)


def flips(size, bit):
    return [(i, i ^ bit) for i in range(size)]


def on_device(images, gauge_pixel, row_mask, gauge_counts, targets, theta, amplitude, damping):
    nrows = lax.axis_size("rows")
    ncols = lax.axis_size("cols")
    row = lax.axis_index("rows")
    column = lax.axis_index("cols")
    slots = gauge_pixel.shape[0]
    share = slots // ncols
    chans, basis = theta.shape
    params = chans * basis
    if ncols == 2:
        half, quarter = column, row % 2
    else:
        half, quarter = column // 2 % 2, column % 2
    place = jnp.stack([half, quarter, column]).astype(jnp.int32)
    shape = jax.ShapeDtypeStruct
    keep, send, slope, phi, resid = pl.pallas_call(
        functools.partial(front, ncols),
        out_shape=[
            shape((PACK, 128), F32),
            shape((PACK, 128), F32),
            shape((chans, share), F32),
            shape((basis, share), F32),
            shape((1, share), F32),
        ],
        in_specs=[SMEM, SMEM] + [VMEM] * 6,
        out_specs=[VMEM] * 5,
        scratch_shapes=[
            pltpu.VMEM((basis, 128, 512), BF16),
            pltpu.VMEM((params, slots), BF16),
            pltpu.VMEM((params, slots), BF16),
            pltpu.VMEM((basis, slots), F32),
            pltpu.VMEM((chans, slots), F32),
            pltpu.VMEM((chans, slots), F32),
            pltpu.VMEM((1, slots), F32),
        ],
        compiler_params=pltpu.CompilerParams(vmem_limit_bytes=40 * 2**20),
        name="front",
    )(
        place,
        gauge_counts,
        images.reshape(-1, images.shape[2]),
        gauge_pixel.reshape(1, slots),
        row_mask.reshape(1, slots),
        targets.reshape(1, slots),
        theta,
        amplitude.reshape(1, chans),
    )

    bit = 1
    if ncols == 2:
        keep = keep + lax.ppermute(send, "rows", flips(nrows, 1))
        bit = 2
    while bit < nrows:
        keep = keep + lax.ppermute(keep, "rows", flips(nrows, bit))
        bit *= 2
    if ncols == 2:
        other_half = lax.ppermute(keep, "cols", flips(ncols, 1))
        other_quarter = lax.ppermute(keep, "rows", flips(nrows, 1))
        other_both = lax.ppermute(other_half, "rows", flips(nrows, 1))
    else:
        other_half = lax.ppermute(keep, "cols", flips(ncols, 2))
        other_quarter = lax.ppermute(keep, "cols", flips(ncols, 1))
        other_both = lax.ppermute(other_half, "cols", flips(ncols, 1))

    r_factor, new_theta, predicted = pl.pallas_call(
        back,
        out_shape=[
            shape((params, params), F32),
            shape((chans, basis), F32),
            shape((1, share), F32),
        ],
        in_specs=[SMEM, SMEM] + [VMEM] * 8,
        out_specs=[VMEM] * 3,
        scratch_shapes=[
            pltpu.VMEM((4, PACK, 128), F32),
            pltpu.VMEM((params, params), F32),
            pltpu.VMEM((params // 128, params, 128), F32),
            pltpu.VMEM((params // 128 + 1, params, 128), F32),
            pltpu.VMEM((params // BLK, BLK, BLK), F32),
            pltpu.VMEM((params, 128), F32),
        ],
        compiler_params=pltpu.CompilerParams(vmem_limit_bytes=40 * 2**20),
        name="back",
    )(
        place,
        damping.reshape(1, 1),
        keep,
        other_half,
        other_quarter,
        other_both,
        slope,
        phi,
        resid,
        theta,
    )
    return r_factor, new_theta, predicted.reshape(share)


def solution(mesh):
    return jax.shard_map(
        on_device,
        mesh=mesh,
        in_specs=(P("rows", None, None), P("rows"), P("rows"), P("rows"), P("rows"), P(), P(), P()),
        out_specs=(P(), P(), P(("rows", "cols"))),
        check_vma=False,
    )
```

profile of v0, /device:TPU:0, one launch (start us, length us, event | category | flops | bytes accessed | tf_op | source)
XLA Modules:
  0.0 60.2 jit_solution(4703590848041475802)
XLA Ops:
  0.6 0.0 copy-start.5
  1.3 0.0 copy-done.5
  1.3 0.0 copy-start.3
  1.3 0.1 copy.11.theta_ref
  1.4 0.0 copy-start.2
  1.4 0.0 copy-start.1
  1.4 0.1 pad_add_fusion.place_ref
  1.5 0.0 copy-start.4
  1.5 0.5 copy-done.3
  2.0 0.1 copy-done.2
  2.1 0.0 copy-done.1
  2.1 0.0 copy-done.4
  2.2 0.0 copy-start
  2.2 0.9 %copy-done = f32[8,32,128]{2,1,0:T(8,128)S(1)} copy-done((f32[8,32,128]{2,1,0:T(8,128)S(1)}, f32[8,32,128]{2,1,0:T(8,128)}, u32[]{:S(2)}) %copy-start) | copy-done | bytes 131096
  3.1 7.9 %front.1 = (f32[168,128]{1,0:T(8,128)S(1)}, f32[168,128]{1,0:T(8,128)S(1)}, f32[64,1024]{1,0:T(8,128)S(1)}, f32[8,1024]{1,0:T(8,128)S(1)}, f32[1,1024]{1,0:T(1,128)S(1)}) custom-call(s32[3]{0:T(128)S(1)} %pad_add_fusion.place_ref, s32[1]{0:T(128)S(6)} %copy.14.count_ref, f32[256,128]{1,0:T(8,128)S(1)} %bitcast.10, s32[1,2048]{1,0:T(1,128)S(1)} %bitcast.11, ...), custom_call_target="tpu_custom_call" | custom-call | tf_op jit(solution)/shard_map/front/pallas_call | solution.py:379
  11.0 0.5 collective-permute-start
  11.5 0.9 %collective-permute-done = f32[168,128]{1,0:T(8,128)S(1)} collective-permute-done((f32[168,128]{1,0:T(8,128)S(1)}, f32[168,128]{1,0:T(8,128)S(1)}, u32[]{:S(2)}, u32[]{:S(2)}) %collective-permute-start) | collective-permute-done | bytes 86048 | tf_op jit(solution)/shard_map/ppermute | solution.py:414
  12.4 2.9 %collective-permute-start.1 = (f32[168,128]{1,0:T(8,128)S(1)}, f32[168,128]{1,0:T(8,128)S(1)}, u32[]{:S(2)}, u32[]{:S(2)}) collective-permute-start(f32[168,128]{1,0:T(8,128)S(1)} %add.17), channel_id=1, source_target_pairs={{0,4},{2,6},{4,0},{6,2},{8,12},{10,14},{12,8},{14,10},{16,20},{18,... | collective-permute-start | bytes 258056 | tf_op jit(solution)/shard_map/ppermute | solution.py:417
  15.3 2.9 %collective-permute-done.1 = f32[168,128]{1,0:T(8,128)S(1)} collective-permute-done((f32[168,128]{1,0:T(8,128)S(1)}, f32[168,128]{1,0:T(8,128)S(1)}, u32[]{:S(2)}, u32[]{:S(2)}) %collective-permute-start.1) | collective-permute-done | bytes 86048 | tf_op jit(solution)/shard_map/ppermute | solution.py:417
  18.2 1.9 %collective-permute-start.2 = (f32[168,128]{1,0:T(8,128)S(1)}, f32[168,128]{1,0:T(8,128)S(1)}, u32[]{:S(2)}, u32[]{:S(2)}) collective-permute-start(f32[168,128]{1,0:T(8,128)S(1)} %add.18), channel_id=1, source_target_pairs={{0,8},{2,10},{4,12},{6,14},{8,0},{10,2},{12,4},{14,6},{16,24},{18,... | collective-permute-start | bytes 258056 | tf_op jit(solution)/shard_map/ppermute | solution.py:417
  20.1 2.7 %collective-permute-done.2 = f32[168,128]{1,0:T(8,128)S(1)} collective-permute-done((f32[168,128]{1,0:T(8,128)S(1)}, f32[168,128]{1,0:T(8,128)S(1)}, u32[]{:S(2)}, u32[]{:S(2)}) %collective-permute-start.2) | collective-permute-done | bytes 86048 | tf_op jit(solution)/shard_map/ppermute | solution.py:417
  22.8 2.9 %collective-permute-start.3 = (f32[168,128]{1,0:T(8,128)S(1)}, f32[168,128]{1,0:T(8,128)S(1)}, u32[]{:S(2)}, u32[]{:S(2)}) collective-permute-start(f32[168,128]{1,0:T(8,128)S(1)} %add.19), channel_id=1, source_target_pairs={{0,16},{2,18},{4,20},{6,22},{8,24},{10,26},{12,28},{14,30},{16,0},... | collective-permute-start | bytes 258056 | tf_op jit(solution)/shard_map/ppermute | solution.py:417
  25.7 2.6 %collective-permute-done.3 = f32[168,128]{1,0:T(8,128)S(1)} collective-permute-done((f32[168,128]{1,0:T(8,128)S(1)}, f32[168,128]{1,0:T(8,128)S(1)}, u32[]{:S(2)}, u32[]{:S(2)}) %collective-permute-start.3) | collective-permute-done | bytes 86048 | tf_op jit(solution)/shard_map/ppermute | solution.py:417
  28.2 1.8 %collective-permute-start.4 = (f32[168,128]{1,0:T(8,128)S(1)}, f32[168,128]{1,0:T(8,128)S(1)}, u32[]{:S(2)}, u32[]{:S(2)}) collective-permute-start(f32[168,128]{1,0:T(8,128)S(1)} %add.20.q0_ref), channel_id=1, source_target_pairs={{0,1},{1,0},{2,3},{3,2},{4,5},{5,4},{6,7},{7,6},{8,9},{9,8},{10,11... | collective-permute-start | bytes 258056 | tf_op jit(solution)/shard_map/ppermute | solution.py:420
  30.0 0.0 collective-permute-start.5
  30.0 2.8 %collective-permute-done.4.q1_ref = f32[168,128]{1,0:T(8,128)S(1)} collective-permute-done((f32[168,128]{1,0:T(8,128)S(1)}, f32[168,128]{1,0:T(8,128)S(1)}, u32[]{:S(2)}, u32[]{:S(2)}) %collective-permute-start.4) | collective-permute-done | bytes 86048 | tf_op jit(solution)/shard_map/ppermute | solution.py:420
  32.8 0.0 collective-permute-start.6
  33.5 0.0 collective-permute-done.5.q2_ref
  33.5 0.6 %collective-permute-done.6.q3_ref = f32[168,128]{1,0:T(8,128)S(1)} collective-permute-done((f32[168,128]{1,0:T(8,128)S(1)}, f32[168,128]{1,0:T(8,128)S(1)}, u32[]{:S(2)}, u32[]{:S(2)}) %collective-permute-start.6) | collective-permute-done | bytes 86048 | tf_op jit(solution)/shard_map/ppermute | solution.py:422
  34.1 25.5 %back.1 = (f32[512,512]{1,0:T(8,128)}, f32[64,8]{1,0:T(8,128)S(1)}, f32[1,1024]{1,0:T(1,128)}) custom-call(s32[3]{0:T(128)S(1)} %pad_add_fusion.place_ref, f32[1,1]{1,0:T(1,128)} %bitcast.9.damping_ref, f32[168,128]{1,0:T(8,128)S(1)} %add.20.q0_ref, f32[168,128]{1,0:T(8,128)S(1)} %collective-permute-done.4.q1_ref, ...), custom_call_target="tpu_custom_call" | custom-call | tf_op jit(solution)/shard_map/back/pallas_call | solution.py:428
  59.5 0.7 %copy.13 = f32[64,8]{0,1:T(8,128)} copy(f32[64,8]{1,0:T(8,128)S(1)} %get-tuple-element.20) | data formatting | bytes 4096
  (4 shorter events, 0.1 us)
Async XLA Ops:
  0.6 0.7 %copy-start.5 = (f32[64,8]{0,1:T(8,128)S(1)}, f32[64,8]{0,1:T(8,128)}, u32[]{:S(2)}) copy-start(f32[64,8]{0,1:T(8,128)} %param.13) | copy-start | bytes 6148
  1.3 0.7 %copy-start.3 = (f32[2048]{0:T(1024)S(1)}, f32[2048]{0:T(1024)}, u32[]{:S(2)}) copy-start(f32[2048]{0:T(1024)} %param.12) | copy-start | bytes 24580
  1.4 0.7 %copy-start.2 = (s32[2048]{0:T(1024)S(1)}, s32[2048]{0:T(1024)}, u32[]{:S(2)}) copy-start(s32[2048]{0:T(1024)} %param.10) | copy-start | bytes 24580
  1.4 0.7 %copy-start.1 = (s32[2048]{0:T(1024)S(1)}, s32[2048]{0:T(1024)}, u32[]{:S(2)}) copy-start(s32[2048]{0:T(1024)} %param.9) | copy-start | bytes 24580
  1.5 0.7 %copy-start.4 = (f32[64]{0:T(128)S(1)}, f32[64]{0:T(128)}, u32[]{:S(2)}) copy-start(f32[64]{0:T(128)} %param.14) | copy-start | bytes 772
  2.2 0.9 %copy-start = (f32[8,32,128]{2,1,0:T(8,128)S(1)}, f32[8,32,128]{2,1,0:T(8,128)}, u32[]{:S(2)}) copy-start(f32[8,32,128]{2,1,0:T(8,128)} %param.8) | copy-start | bytes 393220
  11.0 1.4 %collective-permute-start = (f32[168,128]{1,0:T(8,128)S(1)}, f32[168,128]{1,0:T(8,128)S(1)}, u32[]{:S(2)}, u32[]{:S(2)}) collective-permute-start(f32[168,128]{1,0:T(8,128)S(1)} %get-tuple-element.12), channel_id=1, source_target_pairs={{0,2},{2,0},{4,6},{6,4},{8,10},{10,8},{12,14},{14,12},{16,18},{18,... | collective-permute-start | bytes 258056 | tf_op jit(solution)/shard_map/ppermute | solution.py:414
  12.4 5.8 %collective-permute-start.1 = (f32[168,128]{1,0:T(8,128)S(1)}, f32[168,128]{1,0:T(8,128)S(1)}, u32[]{:S(2)}, u32[]{:S(2)}) collective-permute-start(f32[168,128]{1,0:T(8,128)S(1)} %add.17), channel_id=1, source_target_pairs={{0,4},{2,6},{4,0},{6,2},{8,12},{10,14},{12,8},{14,10},{16,20},{18,... | collective-permute-start | bytes 258056 | tf_op jit(solution)/shard_map/ppermute | solution.py:417
  18.2 4.6 %collective-permute-start.2 = (f32[168,128]{1,0:T(8,128)S(1)}, f32[168,128]{1,0:T(8,128)S(1)}, u32[]{:S(2)}, u32[]{:S(2)}) collective-permute-start(f32[168,128]{1,0:T(8,128)S(1)} %add.18), channel_id=1, source_target_pairs={{0,8},{2,10},{4,12},{6,14},{8,0},{10,2},{12,4},{14,6},{16,24},{18,... | collective-permute-start | bytes 258056 | tf_op jit(solution)/shard_map/ppermute | solution.py:417
  22.8 5.4 %collective-permute-start.3 = (f32[168,128]{1,0:T(8,128)S(1)}, f32[168,128]{1,0:T(8,128)S(1)}, u32[]{:S(2)}, u32[]{:S(2)}) collective-permute-start(f32[168,128]{1,0:T(8,128)S(1)} %add.19), channel_id=1, source_target_pairs={{0,16},{2,18},{4,20},{6,22},{8,24},{10,26},{12,28},{14,30},{16,0},... | collective-permute-start | bytes 258056 | tf_op jit(solution)/shard_map/ppermute | solution.py:417
  28.2 4.6 %collective-permute-start.4 = (f32[168,128]{1,0:T(8,128)S(1)}, f32[168,128]{1,0:T(8,128)S(1)}, u32[]{:S(2)}, u32[]{:S(2)}) collective-permute-start(f32[168,128]{1,0:T(8,128)S(1)} %add.20.q0_ref), channel_id=1, source_target_pairs={{0,1},{1,0},{2,3},{3,2},{4,5},{5,4},{6,7},{7,6},{8,9},{9,8},{10,11... | collective-permute-start | bytes 258056 | tf_op jit(solution)/shard_map/ppermute | solution.py:420
  30.0 3.4 %collective-permute-start.5 = (f32[168,128]{1,0:T(8,128)S(1)}, f32[168,128]{1,0:T(8,128)S(1)}, u32[]{:S(2)}, u32[]{:S(2)}) collective-permute-start(f32[168,128]{1,0:T(8,128)S(1)} %add.20.q0_ref), channel_id=1, source_target_pairs={{0,2},{2,0},{4,6},{6,4},{8,10},{10,8},{12,14},{14,12},{16,18},{18,... | collective-permute-start | bytes 258056 | tf_op jit(solution)/shard_map/ppermute | solution.py:421
  32.8 1.3 %collective-permute-start.6 = (f32[168,128]{1,0:T(8,128)S(1)}, f32[168,128]{1,0:T(8,128)S(1)}, u32[]{:S(2)}, u32[]{:S(2)}) collective-permute-start(f32[168,128]{1,0:T(8,128)S(1)} %collective-permute-done.4.q1_ref), channel_id=1, source_target_pairs={{0,2},{2,0},{4,6},{6,4},{8,10},{10,8},{12,14},{14,12},{16,18},{18,... | collective-permute-start | bytes 258056 | tf_op jit(solution)/shard_map/ppermute | solution.py:422
where the time goes:
time: 60.5 us; the launch traced here: 60.2 us
  Pallas kernels  33.4 us (55%)
  waiting for transfers between devices  12.4 us (20%)
  starting transfers between devices  9.96 us (16%)
  local copies, waits for them, and re-layouts  2.33 us (4%)
  between operations  1.99 us (3%)
    pallas_call x1, Pallas kernels, on_device(): pl.pallas_call(back, out_shape=[shape((params, params), F32), shape((chan...  25.5 us
    ppermute x3, waiting for transfers between devices, on_device(): keep = keep + lax.ppermute(keep, 'rows', flips(nrows, bit))  8.11 us
    pallas_call x1, Pallas kernels, on_device(): pl.pallas_call(functools.partial(front, ncols), out_shape=[shape((PACK, 1...  7.9 us
    ppermute x3, starting transfers between devices, on_device(): keep = keep + lax.ppermute(keep, 'rows', flips(nrows, bit))  7.67 us
    ppermute x1, waiting for transfers between devices, on_device(): other_half = lax.ppermute(keep, 'cols', flips(ncols, 1))  2.77 us
    unnamed x14, local copies, waits for them, and re-layouts  2.33 us
    ppermute x1, starting transfers between devices, on_device(): other_half = lax.ppermute(keep, 'cols', flips(ncols, 1))  1.78 us
  transfers between devices with their start and end apart: 7, of which 6 were waited for; matrix products, arithmetic and copies ran while one was open for 0% of the time, Pallas kernels for 0%

commit v1 on v0

v1 whole, which is shorter than its diff:
```python
import functools
import math

import jax
import jax.numpy as jnp
from jax import lax
from jax.experimental import pallas as pl
from jax.experimental.pallas import tpu as pltpu
from jax.sharding import PartitionSpec as P

Y_ORDERS = [0, 1, 0, 2, 1, 0, 0, 0]
X_ORDERS = [0, 0, 1, 0, 1, 2, 0, 2]
SIGMAS = [1.5, 1.5, 1.5, 1.5, 1.5, 1.5, 3.0, 3.0]

F32 = jnp.float32
BF16 = jnp.bfloat16
NN = (((1,), (0,)), ((), ()))
NT = (((1,), (1,)), ((), ()))
VMEM = pl.BlockSpec(memory_space=pltpu.VMEM)
HBM = pl.BlockSpec(memory_space=pltpu.HBM)
SMEM = pl.BlockSpec(memory_space=pltpu.SMEM)
PACK = 176
CHUNK = 512
AHEAD = 2
BLK = 64


def iota(shape, dim):
    return lax.broadcasted_iota(jnp.int32, shape, dim)


def kernel_scale(order, width):
    total = 0.0
    for t in range(-12, 13):
        e = math.exp(-t * t / (2.0 * width * width))
        if order == 1:
            e = -t / width**2 * e
        elif order == 2:
            e = (t * t / width**4 - 1.0 / width**2) * e
        total += e * e
    return 1.0 / math.sqrt(total)


def kernel_values(lag, order, width):
    e = jnp.exp(lag * lag * (-1.0 / (2.0 * width * width)))
    if order == 1:
        e = lag * (-1.0 / width**2) * e
    elif order == 2:
        e = (lag * lag * (1.0 / width**4) - 1.0 / width**2) * e
    return e * kernel_scale(order, width)


def split(a):
    hi = a.astype(BF16)
    return hi, (a - hi.astype(F32)).astype(BF16)


def dot(a, b, dims=NN):
    return lax.dot_general(a, b, dims, preferred_element_type=F32)


def dot3(a, b, dims=NN):
    ah, al = a if isinstance(a, tuple) else split(a)
    bh, bl = b if isinstance(b, tuple) else split(b)
    return dot(ah, bh, dims) + (dot(ah, bl, dims) + dot(al, bh, dims))


def dot_full(a, b, dims=NN):
    return lax.dot_general(
        a, b, dims, precision=lax.Precision.HIGHEST, preferred_element_type=F32
    )


mm = dot_full


def places(ncols):
    column = lax.axis_index("cols")
    if ncols == 2:
        return column, lax.axis_index("rows") & 1, column
    return (column >> 1) & 1, column & 1, column


def front(
    ncols,
    count_ref,
    img_hbm,
    pix_hbm,
    mask_hbm,
    target_hbm,
    theta_hbm,
    amp_hbm,
    keep_ref,
    send_ref,
    slope_ref,
    phi_ref,
    resid_ref,
    img_ref,
    pix_ref,
    mask_ref,
    target_ref,
    theta_ref,
    amp_ref,
    pick_ref,
    feat_ref,
    jac_ref,
    all_phi_ref,
    all_sr_ref,
    all_slope_ref,
    all_resid_ref,
    sem,
):
    pairs = [
        (img_hbm, img_ref),
        (pix_hbm, pix_ref),
        (theta_hbm, theta_ref),
        (amp_hbm, amp_ref),
        (mask_hbm, mask_ref),
        (target_hbm, target_ref),
    ]
    copies = [pltpu.make_async_copy(a, b, sem.at[i]) for i, (a, b) in enumerate(pairs)]
    for copy in copies:
        copy.start()
    half, quarter, column = places(ncols)
    count = count_ref[0]
    slots = pix_ref.shape[1]
    rows, breadth = img_ref.shape
    height = 32
    basis, chans = theta_ref.shape
    params = basis * chans

    kinds = sorted(set(zip(Y_ORDERS, SIGMAS)))
    tables = []
    for order, width in kinds:
        lag = ((iota((height, breadth), 1) & (height - 1)) - iota((height, breadth), 0)).astype(F32)
        table = kernel_values(lag, order, width)
        wide = jnp.concatenate([table] * (rows // height), 0)
        wide = jnp.concatenate([wide] * (rows // breadth), 1)
        same = (iota((rows, rows), 0) // height) == (iota((rows, rows), 1) // height)
        tables.append(split(jnp.where(same, wide, 0.0)))
    lag = (iota((breadth, breadth), 0) - iota((breadth, breadth), 1)).astype(F32)
    rights = [split(kernel_values(lag, X_ORDERS[k], SIGMAS[k])) for k in range(basis)]
    copies[1].wait()
    chunk = min(CHUNK, slots)
    for start in range(0, slots, chunk):
        row = pix_ref[:, start : start + chunk] // breadth
        pick = jnp.where(iota((rows, chunk), 0) == row, 1.0, 0.0).astype(BF16)
        pick_ref[:rows, start : start + chunk] = pick
        pick_ref[rows:, start : start + chunk] = pick
    copies[0].wait()
    image_t = split(img_ref[...].T)
    lefts = {kind: split(dot3(image_t, table)) for kind, table in zip(kinds, tables)}
    for k in range(basis):
        hi, lo = split(dot3(rights[k], lefts[Y_ORDERS[k], SIGMAS[k]]))
        feat_ref[k * breadth : (k + 1) * breadth, :rows] = hi
        feat_ref[k * breadth : (k + 1) * breadth, rows:] = lo

    for copy in copies[2:]:
        copy.wait()
    theta = theta_ref[...].T
    diag = iota((chans, chans), 0) == iota((chans, chans), 1)
    amp = jnp.sum(jnp.where(diag, amp_ref[...], 0.0), axis=1, keepdims=True)

    live_total = jnp.zeros((1, 1), F32)
    for start in range(0, slots, chunk):
        at = slice(start, start + chunk)
        pick_col = iota((breadth, chunk), 0) == pix_ref[:, at] & (breadth - 1)
        phis = []
        for k in range(basis):
            found = dot(feat_ref[k * breadth : (k + 1) * breadth], pick_ref[:, at])
            phis.append(jnp.sum(jnp.where(pick_col, found, 0.0), axis=0, keepdims=True))
        phi = jnp.concatenate(phis, 0)
        all_phi_ref[:, at] = phi
        slot = iota((1, chunk), 1) + start
        live = jnp.where((slot < count) & (mask_ref[:, at] == 1), 1.0, 0.0)
        live_total = live_total + jnp.sum(live, axis=1, keepdims=True)
        z = theta[:, 0:1] * phis[0]
        for k in range(1, basis):
            z = z + theta[:, k : k + 1] * phis[k]
        act = jnp.tanh(z)
        model = jnp.sum(amp * act, axis=0, keepdims=True)
        resid = live * (model - target_ref[:, at])
        slope = (live * amp) * (1.0 - act * act)
        all_resid_ref[:, at] = resid
        all_slope_ref[:, at] = slope
        all_sr_ref[:, at] = slope * resid
        for k in range(basis):
            hi, lo = split(slope * phis[k])
            place = ((k + (basis // 2) * half) % basis) * chans
            jac_ref[pl.ds(pl.multiple_of(place, chans), chans), at] = hi
            jac_ref[pl.ds(pl.multiple_of(params + place, chans), chans), at] = lo

    own = slots // ncols
    mine = pl.ds(pl.multiple_of(column * own, own), own)
    slope_ref[...] = all_slope_ref[:, mine]
    phi_ref[...] = all_phi_ref[:, mine]
    resid_ref[...] = all_resid_ref[:, mine]

    grad = dot3(all_phi_ref[...], all_sr_ref[...], NT)

    four = basis // 2 * chans
    both = dot(jac_ref[:four], jac_ref[...], NT)
    low = dot(jac_ref[params : params + four], jac_ref[:params], NT)
    gram = both[:, :params] + (both[:, params:] + low)
    r = iota((chans, 128), 0)
    c = iota((chans, 128), 1) & (chans - 1)
    packs = []
    for part in range(2):
        tiles = [
            [
                gram[
                    (2 * part + e) * chans : (2 * part + e + 1) * chans,
                    (part + i) * 128 : (part + i + 1) * 128,
                ]
                for i in range(3)
            ]
            for e in range(2)
        ]
        spare = jnp.where(iota((chans, 128), 1) < chans, tiles[0][2], tiles[1][0])
        folds = []
        lost = []
        for one, two in (
            (tiles[0][0], tiles[0][1]),
            (tiles[1][1], tiles[1][2]),
            (spare, pltpu.roll(spare, chans, 1)),
        ):
            folds.append(jnp.where(r >= c, one, two))
            lost.append(jnp.sum(jnp.where(r == c, two, 0.0), axis=0, keepdims=True))
        last = folds.pop()
        folds.append(jnp.concatenate([last[: chans // 2, :chans], last[chans // 2 :, :chans]], 1))
        wide = jnp.broadcast_to(live_total, (1, 128))
        folds.append(jnp.concatenate(lost + [wide, jnp.zeros((4, 128), F32)], 0))
        folds.append(jnp.concatenate([grad, jnp.zeros((basis, 128 - chans), F32)], 1))
        packs.append(folds)
    at = 0
    for one, two in zip(*packs):
        piece = pl.ds(at, one.shape[0])
        keep_ref[piece, :] = jnp.where(quarter == 0, one, two)
        send_ref[piece, :] = jnp.where(quarter == 0, two, one)
        at += one.shape[0]


def factor_block(tiles, base):
    count = len(tiles)
    tiles = list(tiles)
    sub = iota((8, 128), 0)
    inverses = []

    def spread(x):
        return jnp.broadcast_to(x, (8, 128))

    def column(t, at):
        return spread(tiles[t][:, at : at + 1])

    ahead = {}
    for g in range(count):
        here = range(g, count)
        cols = {
            t: ahead[t] if t in ahead else [column(t, base + 8 * g + m) for m in range(8)]
            for t in here
        }
        ahead = {
            t: [column(t, base + 8 * g + 8 + m) for m in range(8)]
            for t in range(g + 1, min(g + 1 + AHEAD, count))
        }
        kept = jnp.zeros((8, 128), F32)
        for m in range(8):
            inverse = 1.0 / spread(cols[g][m][m : m + 1])
            kept = jnp.where(sub == m, inverse, kept)
            mult = {t: cols[t][m] * inverse for t in here}
            mult[g] = jnp.where(sub > m, mult[g], 0.0)
            for n in range(m + 1, 8):
                pivot = spread(cols[g][n][m : m + 1])
                for t in here:
                    cols[t][n] = cols[t][n] - mult[t] * pivot
            for n in range(8 if ahead else 0):
                pivot = spread(cols[g + 1][m][n : n + 1])
                for t in ahead:
                    ahead[t][n] = ahead[t][n] - mult[t] * pivot
            pivot = spread(tiles[g][m : m + 1])
            for t in here:
                tiles[t] = tiles[t] - mult[t] * pivot
        inverses.append(kept)
    return tiles, inverses


def back(
    ncols,
    damping_ref,
    q0_ref,
    q1_ref,
    q2_ref,
    q3_ref,
    slope_ref,
    phi_ref,
    resid_ref,
    theta_ref,
    r_ref,
    new_theta_ref,
    pred_ref,
    pack_ref,
    plain_ref,
    mixed_ref,
    n_ref,
    t_ref,
    x_ref,
):
    half, quarter, _ = places(ncols)
    basis, chans = theta_ref.shape
    params = chans * basis
    pack_ref[2 * half + quarter] = q0_ref[...]
    pack_ref[2 * (1 - half) + quarter] = q1_ref[...]
    pack_ref[2 * half + (1 - quarter)] = q2_ref[...]
    pack_ref[2 * (1 - half) + (1 - quarter)] = q3_ref[...]

    total = pack_ref[0, PACK - 13 : PACK - 12, :1]
    scale = 1.0 / total
    r = iota((chans, chans), 0)
    c = iota((chans, chans), 1)

    def put(k, l, block):
        plain_ref[k * chans : (k + 1) * chans, l * chans : (l + 1) * chans] = block

    for q in range(4):
        lost = pack_ref[q, PACK - 16 : PACK - 13, :]
        for i in range(2):
            fold = pack_ref[q, i * chans : (i + 1) * chans, :]
            turned = fold.T
            k = 2 * q + i
            for e in range(2):
                lane = slice(e * chans, (e + 1) * chans)
                f, ft = fold[:, lane], turned[lane]
                second = jnp.where(r == c, lost[i : i + 1, lane], jnp.where(r < c, f, ft))
                for d, block in ((i + e, jnp.where(r >= c, f, ft)), (i + e + 2, second)):
                    l = (k + d) % basis
                    put(k, l, block)
                    if d not in (0, basis // 2):
                        put(l, k, block)
        last = pack_ref[q, 2 * chans : 2 * chans + chans // 2, :]
        f = jnp.concatenate([last[:, :chans], last[:, chans:]], 0)
        ft = f.T
        put(2 * q, (2 * q + basis // 2) % basis, jnp.where(r >= c, f, ft))
        second = jnp.where(r == c, lost[2:, :chans], jnp.where(r < c, f, ft))
        put(2 * q + 1, 2 * q + 1, second)
    tiles = params // 128
    per = 128 // chans
    for k in range(basis):
        for b in range(tiles):
            mixed_ref[b, pl.ds(k, chans, stride=basis), :] = plain_ref[
                k * chans : (k + 1) * chans, b * 128 : (b + 1) * 128
            ]
    for a in range(tiles):
        for b in range(tiles):
            t = mixed_ref[b, a * 128 : (a + 1) * 128, :].T * scale
            for e in range(per):
                n_ref[a, pl.ds(b * per + e, chans, stride=basis), :] = t[
                    e * chans : (e + 1) * chans
                ]
    grad = (pack_ref[0, PACK - 8 :, :] * scale).T[:chans]
    for k in range(basis):
        n_ref[tiles, pl.ds(k, chans, stride=basis), :] = jnp.broadcast_to(
            grad[:, k : k + 1], (chans, 128)
        )

    damping = damping_ref[0, 0]
    for t in range(tiles):
        at = slice(t * 128, (t + 1) * 128)
        spot = iota((128, 128), 0) == iota((128, 128), 1)
        n_ref[t, at, :] = n_ref[t, at, :] + jnp.where(spot, damping, 0.0)

    lane = iota((BLK, 128), 1)
    sub = iota((BLK, 128), 0)
    zeros = jnp.zeros((BLK, 128), F32)

    def load(at, first):
        return jnp.concatenate([n_ref[t, at, :] for t in range(first, tiles + 1)], 1)

    def factor(block, base):
        eye = jnp.where(lane - (BLK - base) == sub, 1.0, 0.0)
        whole = jnp.where((lane >= base) & (lane < base + BLK), block, eye)
        parts, inverses = factor_block([whole[8 * t : 8 * t + 8] for t in range(BLK // 8)], base)
        return jnp.concatenate([p * (i * lax.rsqrt(i)) for p, i in zip(parts, inverses)], 0)

    for j in range(tiles):
        top = slice(j * 128, j * 128 + BLK)
        low = slice(j * 128 + BLK, (j + 1) * 128)
        if j:
            r_ref[j * 128 : (j + 1) * 128, : j * 128] = jnp.zeros((128, j * 128), F32)
        w0 = factor(n_ref[j, top, :], 0)
        inv0 = jnp.where(lane >= BLK, w0, 0.0)
        first = mm(inv0, jnp.concatenate([zeros, n_ref[j, top, :]], 0))
        r_ref[top, j * 128 : (j + 1) * 128] = jnp.where(
            lane >= BLK, first, jnp.where(lane >= sub, w0, 0.0)
        )
        cross = first[:, BLK:].T
        w1 = factor(n_ref[j, low, :] - mm(cross, first), BLK)
        r_ref[low, j * 128 : (j + 1) * 128] = jnp.where(lane - BLK >= sub, w1, 0.0)
        inv1 = w1[:, :BLK]
        over0 = load(top, j + 1)
        rest0 = mm(inv0, jnp.concatenate([jnp.zeros(over0.shape, F32), over0], 0))
        rest1 = mm(inv1, load(low, j + 1) - mm(cross, rest0))
        rest = jnp.concatenate([rest0, rest1], 0)
        if j + 1 < tiles:
            r_ref[j * 128 : (j + 1) * 128, (j + 1) * 128 :] = rest[:, :-128]
            for i in range(j + 1, tiles):
                begin = (i - j - 1) * 128
                turned = rest[:, begin : begin + 128].T
                update = mm(turned, rest[:, begin:])
                at = slice(i * 128, (i + 1) * 128)
                for t in range(i, tiles + 1):
                    n_ref[t, at, :] = n_ref[t, at, :] - update[:, (t - i) * 128 : (t - i + 1) * 128]
        turn1 = mm(w1.T[:BLK], rest1)
        whole0 = mm(w0.T[BLK:], jnp.concatenate([first, rest0], 1))
        link = jnp.where(lane >= BLK, whole0[:, :128], 0.0)
        turn0 = whole0[:, 128:] - mm(
            link, jnp.concatenate([jnp.zeros(turn1.shape, F32), turn1], 0)
        )
        turn = jnp.concatenate([turn0, turn1], 0)
        for t in range(j + 1, tiles + 1):
            t_ref[j, t] = turn[:, (t - j - 1) * 128 : (t - j) * 128]

    for j in reversed(range(tiles)):
        x = t_ref[j, tiles]
        if j + 1 < tiles:
            x = x - mm(
                jnp.concatenate([t_ref[j, t] for t in range(j + 1, tiles)], 1),
                x_ref[(j + 1) * 128 :, :],
            )
        x_ref[j * 128 : (j + 1) * 128, :] = x

    lane = iota((chans, 128), 1)
    weight = jnp.zeros(slope_ref.shape, F32)
    move = jnp.zeros((chans, 128), F32)
    width = slope_ref.shape[1]
    for k in range(basis):
        step = -x_ref[pl.ds(k, chans, stride=basis), :]
        move = jnp.where(lane == k, step, move)
        wide = jnp.concatenate([step] * (width // 128), 1)
        weight = weight + wide * phi_ref[k : k + 1, :]
    new_theta_ref[...] = theta_ref[...] + move.T[:basis]
    pred_ref[...] = resid_ref[...] + jnp.sum(slope_ref[...] * weight, axis=0, keepdims=True)


def flips(size, bit):
    return [(i, i ^ bit) for i in range(size)]


def on_device(images, gauge_pixel, row_mask, gauge_counts, targets, theta, amplitude, damping):
    nrows = lax.axis_size("rows")
    ncols = lax.axis_size("cols")
    slots = gauge_pixel.shape[0]
    share = slots // ncols
    chans, basis = theta.shape
    params = chans * basis
    breadth = images.shape[2]
    pixel_rows = images.shape[0] * images.shape[1]
    theta_t = theta.T
    shape = jax.ShapeDtypeStruct
    keep, send, slope, phi, resid = pl.pallas_call(
        functools.partial(front, ncols),
        out_shape=[
            pltpu.VMEM((PACK, 128), F32),
            pltpu.VMEM((PACK, 128), F32),
            pltpu.VMEM((chans, share), F32),
            pltpu.VMEM((basis, share), F32),
            pltpu.VMEM((1, share), F32),
        ],
        in_specs=[SMEM] + [HBM] * 6,
        out_specs=[VMEM] * 5,
        scratch_shapes=[
            pltpu.VMEM((pixel_rows, breadth), F32),
            pltpu.VMEM((1, slots), jnp.int32),
            pltpu.VMEM((1, slots), jnp.int32),
            pltpu.VMEM((1, slots), F32),
            pltpu.VMEM((basis, chans), F32),
            pltpu.VMEM((1, chans), F32),
            pltpu.VMEM((2 * pixel_rows, slots), BF16),
            pltpu.VMEM((basis * breadth, 2 * pixel_rows), BF16),
            pltpu.VMEM((2 * params, slots), BF16),
            pltpu.VMEM((basis, slots), F32),
            pltpu.VMEM((chans, slots), F32),
            pltpu.VMEM((chans, slots), F32),
            pltpu.VMEM((1, slots), F32),
            pltpu.SemaphoreType.DMA((6,)),
        ],
        compiler_params=pltpu.CompilerParams(vmem_limit_bytes=60 * 2**20),
        name="front",
    )(
        gauge_counts,
        images.reshape(pixel_rows, breadth),
        gauge_pixel.reshape(1, slots),
        row_mask.reshape(1, slots),
        targets.reshape(1, slots),
        theta_t,
        amplitude.reshape(1, chans),
    )

    bit = 1
    if ncols == 2:
        keep = keep + lax.ppermute(send, "rows", flips(nrows, 1))
        bit = 2
    while bit < nrows:
        keep = keep + lax.ppermute(keep, "rows", flips(nrows, bit))
        bit *= 2
    if ncols == 2:
        other_half = lax.ppermute(keep, "cols", flips(ncols, 1))
        other_quarter = lax.ppermute(keep, "rows", flips(nrows, 1))
        other_both = lax.ppermute(other_half, "rows", flips(nrows, 1))
    else:
        other_half = lax.ppermute(keep, "cols", flips(ncols, 2))
        other_quarter = lax.ppermute(keep, "cols", flips(ncols, 1))
        other_both = lax.ppermute(other_half, "cols", flips(ncols, 1))

    r_factor, new_theta, predicted = pl.pallas_call(
        functools.partial(back, ncols),
        out_shape=[
            shape((params, params), F32),
            shape((basis, chans), F32),
            shape((1, share), F32),
        ],
        in_specs=[SMEM] + [VMEM] * 8,
        out_specs=[VMEM] * 3,
        scratch_shapes=[
            pltpu.VMEM((4, PACK, 128), F32),
            pltpu.VMEM((params, params), F32),
            pltpu.VMEM((params // 128, params, 128), F32),
            pltpu.VMEM((params // 128 + 1, params, 128), F32),
            pltpu.VMEM((params // 128, params // 128 + 1, 128, 128), F32),
            pltpu.VMEM((params, 128), F32),
        ],
        compiler_params=pltpu.CompilerParams(vmem_limit_bytes=40 * 2**20),
        name="back",
    )(
        damping.reshape(1, 1),
        keep,
        other_half,
        other_quarter,
        other_both,
        slope,
        phi,
        resid,
        theta_t,
    )
    return r_factor, new_theta.T, predicted.reshape(share)


def solution(mesh):
    return jax.shard_map(
        on_device,
        mesh=mesh,
        in_specs=(P("rows", None, None), P("rows"), P("rows"), P("rows"), P("rows"), P(), P(), P()),
        out_specs=(P(), P(), P(("rows", "cols"))),
        check_vma=False,
    )
```

time: 60.5 us -> 49.4 us (0.82)
  Pallas kernels: 33.4 us -> 24.2 us
  local copies, waits for them, and re-layouts: 2.33 us -> 0.06 us
    pallas_call x2, Pallas kernels: 33.4 us -> 24.2 us  [the longest x1 16.4 us: on_device(): pl.pallas_call(functools.partial(back, ncols), out_shape=[shape((params,...]
    unnamed x14 -> x2, local copies, waits for them, and re-layouts: 2.33 us -> 0.06 us
where the time goes in v1:
time: 49.4 us; the launch traced here: 48.9 us
  Pallas kernels  24.2 us (49%)
  waiting for transfers between devices  12.6 us (26%)
  starting transfers between devices  10 us (20%)
  between operations  1.97 us (4%)
    pallas_call x1, Pallas kernels, on_device(): pl.pallas_call(functools.partial(back, ncols), out_shape=[shape((params,...  16.4 us
    ppermute x3, waiting for transfers between devices, on_device(): keep = keep + lax.ppermute(keep, 'rows', flips(nrows, bit))  8.27 us
    pallas_call x1, Pallas kernels, on_device(): pl.pallas_call(functools.partial(front, ncols), out_shape=[pltpu.VMEM((PA...  7.83 us
    ppermute x3, starting transfers between devices, on_device(): keep = keep + lax.ppermute(keep, 'rows', flips(nrows, bit))  7.69 us
    ppermute x1, waiting for transfers between devices, on_device(): other_half = lax.ppermute(keep, 'cols', flips(ncols, 1))  2.79 us
    ppermute x1, starting transfers between devices, on_device(): other_half = lax.ppermute(keep, 'cols', flips(ncols, 1))  1.8 us
  transfers between devices with their start and end apart: 7, of which 6 were waited for; matrix products, arithmetic and copies ran while one was open for 0% of the time, Pallas kernels for 0%

profile of v1, /device:TPU:0, one launch (start us, length us, event | category | flops | bytes accessed | tf_op | source)
XLA Modules:
  0.0 48.9 jit_solution(10488601764493030686)
XLA Ops:
  1.3 7.8 %front.1 = (f32[176,128]{1,0:T(8,128)S(1)}, f32[176,128]{1,0:T(8,128)S(1)}, f32[64,1024]{1,0:T(8,128)S(1)}, f32[8,1024]{1,0:T(8,128)S(1)}, f32[1,1024]{1,0:T(1,128)S(1)}) custom-call(s32[1]{0:T(128)S(6)} %copy.11.count_ref, f32[256,128]{1,0:T(8,128)} %bitcast.12, s32[1,2048]{1,0:T(1,128)} %bitcast.13, s32[1,2048]{1,0:T(1,128)} %bitcast.14, ...), custom_call_target="tpu_custom_call" | custom-call | tf_op jit(solution)/shard_map/front/pallas_call | solution.py:459
  9.1 0.5 %collective-permute-start = (f32[176,128]{1,0:T(8,128)S(1)}, f32[176,128]{1,0:T(8,128)S(1)}, u32[]{:S(2)}, u32[]{:S(2)}) collective-permute-start(f32[176,128]{1,0:T(8,128)S(1)} %get-tuple-element.12), channel_id=1, source_target_pairs={{0,2},{2,0},{4,6},{6,4},{8,10},{10,8},{12,14},{14,12},{16,18},{18,... | collective-permute-start | bytes 270344 | tf_op jit(solution)/shard_map/ppermute | solution.py:500
  9.6 0.9 %collective-permute-done = f32[176,128]{1,0:T(8,128)S(1)} collective-permute-done((f32[176,128]{1,0:T(8,128)S(1)}, f32[176,128]{1,0:T(8,128)S(1)}, u32[]{:S(2)}, u32[]{:S(2)}) %collective-permute-start) | collective-permute-done | bytes 90144 | tf_op jit(solution)/shard_map/ppermute | solution.py:500
  10.6 2.9 %collective-permute-start.1 = (f32[176,128]{1,0:T(8,128)S(1)}, f32[176,128]{1,0:T(8,128)S(1)}, u32[]{:S(2)}, u32[]{:S(2)}) collective-permute-start(f32[176,128]{1,0:T(8,128)S(1)} %add.12), channel_id=1, source_target_pairs={{0,4},{2,6},{4,0},{6,2},{8,12},{10,14},{12,8},{14,10},{16,20},{18,... | collective-permute-start | bytes 270344 | tf_op jit(solution)/shard_map/ppermute | solution.py:503
  13.5 2.9 %collective-permute-done.1 = f32[176,128]{1,0:T(8,128)S(1)} collective-permute-done((f32[176,128]{1,0:T(8,128)S(1)}, f32[176,128]{1,0:T(8,128)S(1)}, u32[]{:S(2)}, u32[]{:S(2)}) %collective-permute-start.1) | collective-permute-done | bytes 90144 | tf_op jit(solution)/shard_map/ppermute | solution.py:503
  16.5 1.9 %collective-permute-start.2 = (f32[176,128]{1,0:T(8,128)S(1)}, f32[176,128]{1,0:T(8,128)S(1)}, u32[]{:S(2)}, u32[]{:S(2)}) collective-permute-start(f32[176,128]{1,0:T(8,128)S(1)} %add.13), channel_id=1, source_target_pairs={{0,8},{2,10},{4,12},{6,14},{8,0},{10,2},{12,4},{14,6},{16,24},{18,... | collective-permute-start | bytes 270344 | tf_op jit(solution)/shard_map/ppermute | solution.py:503
  18.3 2.7 %collective-permute-done.2 = f32[176,128]{1,0:T(8,128)S(1)} collective-permute-done((f32[176,128]{1,0:T(8,128)S(1)}, f32[176,128]{1,0:T(8,128)S(1)}, u32[]{:S(2)}, u32[]{:S(2)}) %collective-permute-start.2) | collective-permute-done | bytes 90144 | tf_op jit(solution)/shard_map/ppermute | solution.py:503
  21.1 2.9 %collective-permute-start.3 = (f32[176,128]{1,0:T(8,128)S(1)}, f32[176,128]{1,0:T(8,128)S(1)}, u32[]{:S(2)}, u32[]{:S(2)}) collective-permute-start(f32[176,128]{1,0:T(8,128)S(1)} %add.14), channel_id=1, source_target_pairs={{0,16},{2,18},{4,20},{6,22},{8,24},{10,26},{12,28},{14,30},{16,0},... | collective-permute-start | bytes 270344 | tf_op jit(solution)/shard_map/ppermute | solution.py:503
  24.0 2.6 %collective-permute-done.3 = f32[176,128]{1,0:T(8,128)S(1)} collective-permute-done((f32[176,128]{1,0:T(8,128)S(1)}, f32[176,128]{1,0:T(8,128)S(1)}, u32[]{:S(2)}, u32[]{:S(2)}) %collective-permute-start.3) | collective-permute-done | bytes 90144 | tf_op jit(solution)/shard_map/ppermute | solution.py:503
  26.6 1.8 %collective-permute-start.4 = (f32[176,128]{1,0:T(8,128)S(1)}, f32[176,128]{1,0:T(8,128)S(1)}, u32[]{:S(2)}, u32[]{:S(2)}) collective-permute-start(f32[176,128]{1,0:T(8,128)S(1)} %add.15.q0_ref), channel_id=1, source_target_pairs={{0,1},{1,0},{2,3},{3,2},{4,5},{5,4},{6,7},{7,6},{8,9},{9,8},{10,11... | collective-permute-start | bytes 270344 | tf_op jit(solution)/shard_map/ppermute | solution.py:506
  28.4 0.0 collective-permute-start.5
  28.4 2.8 %collective-permute-done.4.q1_ref = f32[176,128]{1,0:T(8,128)S(1)} collective-permute-done((f32[176,128]{1,0:T(8,128)S(1)}, f32[176,128]{1,0:T(8,128)S(1)}, u32[]{:S(2)}, u32[]{:S(2)}) %collective-permute-start.4) | collective-permute-done | bytes 90144 | tf_op jit(solution)/shard_map/ppermute | solution.py:506
  31.2 0.0 collective-permute-start.6
  31.8 0.0 copy-start
  31.8 0.0 collective-permute-done.5.q2_ref
  31.9 0.6 %collective-permute-done.6.q3_ref = f32[176,128]{1,0:T(8,128)S(1)} collective-permute-done((f32[176,128]{1,0:T(8,128)S(1)}, f32[176,128]{1,0:T(8,128)S(1)}, u32[]{:S(2)}, u32[]{:S(2)}) %collective-permute-start.6) | collective-permute-done | bytes 90144 | tf_op jit(solution)/shard_map/ppermute | solution.py:508
  32.5 0.1 copy-done
  32.5 16.4 %back.1 = (f32[512,512]{1,0:T(8,128)}, f32[8,64]{1,0:T(8,128)}, f32[1,1024]{1,0:T(1,128)}) custom-call(f32[1,1]{1,0:T(1,128)} %bitcast.9.damping_ref, f32[176,128]{1,0:T(8,128)S(1)} %add.15.q0_ref, f32[176,128]{1,0:T(8,128)S(1)} %collective-permute-done.4.q1_ref, f32[176,128]{1,0:T(8,128)S(1)} %collective-permute-done.5.q2_ref, ...), custom_call_target="tpu_custom_call" | custom-call | tf_op jit(solution)/shard_map/back/pallas_call | solution.py:514
  (4 shorter events, 0.1 us)
Async XLA Ops:
  9.1 1.5 %collective-permute-start = (f32[176,128]{1,0:T(8,128)S(1)}, f32[176,128]{1,0:T(8,128)S(1)}, u32[]{:S(2)}, u32[]{:S(2)}) collective-permute-start(f32[176,128]{1,0:T(8,128)S(1)} %get-tuple-element.12), channel_id=1, source_target_pairs={{0,2},{2,0},{4,6},{6,4},{8,10},{10,8},{12,14},{14,12},{16,18},{18,... | collective-permute-start | bytes 270344 | tf_op jit(solution)/shard_map/ppermute | solution.py:500
  10.6 5.9 %collective-permute-start.1 = (f32[176,128]{1,0:T(8,128)S(1)}, f32[176,128]{1,0:T(8,128)S(1)}, u32[]{:S(2)}, u32[]{:S(2)}) collective-permute-start(f32[176,128]{1,0:T(8,128)S(1)} %add.12), channel_id=1, source_target_pairs={{0,4},{2,6},{4,0},{6,2},{8,12},{10,14},{12,8},{14,10},{16,20},{18,... | collective-permute-start | bytes 270344 | tf_op jit(solution)/shard_map/ppermute | solution.py:503
  16.5 4.6 %collective-permute-start.2 = (f32[176,128]{1,0:T(8,128)S(1)}, f32[176,128]{1,0:T(8,128)S(1)}, u32[]{:S(2)}, u32[]{:S(2)}) collective-permute-start(f32[176,128]{1,0:T(8,128)S(1)} %add.13), channel_id=1, source_target_pairs={{0,8},{2,10},{4,12},{6,14},{8,0},{10,2},{12,4},{14,6},{16,24},{18,... | collective-permute-start | bytes 270344 | tf_op jit(solution)/shard_map/ppermute | solution.py:503
  21.1 5.5 %collective-permute-start.3 = (f32[176,128]{1,0:T(8,128)S(1)}, f32[176,128]{1,0:T(8,128)S(1)}, u32[]{:S(2)}, u32[]{:S(2)}) collective-permute-start(f32[176,128]{1,0:T(8,128)S(1)} %add.14), channel_id=1, source_target_pairs={{0,16},{2,18},{4,20},{6,22},{8,24},{10,26},{12,28},{14,30},{16,0},... | collective-permute-start | bytes 270344 | tf_op jit(solution)/shard_map/ppermute | solution.py:503
  26.6 4.6 %collective-permute-start.4 = (f32[176,128]{1,0:T(8,128)S(1)}, f32[176,128]{1,0:T(8,128)S(1)}, u32[]{:S(2)}, u32[]{:S(2)}) collective-permute-start(f32[176,128]{1,0:T(8,128)S(1)} %add.15.q0_ref), channel_id=1, source_target_pairs={{0,1},{1,0},{2,3},{3,2},{4,5},{5,4},{6,7},{7,6},{8,9},{9,8},{10,11... | collective-permute-start | bytes 270344 | tf_op jit(solution)/shard_map/ppermute | solution.py:506
  28.4 3.5 %collective-permute-start.5 = (f32[176,128]{1,0:T(8,128)S(1)}, f32[176,128]{1,0:T(8,128)S(1)}, u32[]{:S(2)}, u32[]{:S(2)}) collective-permute-start(f32[176,128]{1,0:T(8,128)S(1)} %add.15.q0_ref), channel_id=1, source_target_pairs={{0,2},{2,0},{4,6},{6,4},{8,10},{10,8},{12,14},{14,12},{16,18},{18,... | collective-permute-start | bytes 270344 | tf_op jit(solution)/shard_map/ppermute | solution.py:507
  31.2 1.3 %collective-permute-start.6 = (f32[176,128]{1,0:T(8,128)S(1)}, f32[176,128]{1,0:T(8,128)S(1)}, u32[]{:S(2)}, u32[]{:S(2)}) collective-permute-start(f32[176,128]{1,0:T(8,128)S(1)} %collective-permute-done.4.q1_ref), channel_id=1, source_target_pairs={{0,2},{2,0},{4,6},{6,4},{8,10},{10,8},{12,14},{14,12},{16,18},{18,... | collective-permute-start | bytes 270344 | tf_op jit(solution)/shard_map/ppermute | solution.py:508
  31.8 0.7 %copy-start = (f32[64,8]{0,1:T(8,128)S(1)}, f32[64,8]{0,1:T(8,128)}, u32[]{:S(2)}) copy-start(f32[64,8]{0,1:T(8,128)} %param.13) | copy-start | bytes 6148

commit v2 on v1

--- a/solution.py
+++ b/solution.py
@@ -19,8 +19,9 @@
 VMEM = pl.BlockSpec(memory_space=pltpu.VMEM)
 HBM = pl.BlockSpec(memory_space=pltpu.HBM)
 SMEM = pl.BlockSpec(memory_space=pltpu.SMEM)
-PACK = 176
+PACK = 168
 CHUNK = 512
+PACE = 1
 AHEAD = 2
 BLK = 64
 
@@ -95,6 +96,7 @@
     slope_ref,
     phi_ref,
     resid_ref,
+    theta_out_ref,
     img_ref,
     pix_ref,
     mask_ref,
@@ -157,6 +159,7 @@
 
     for copy in copies[2:]:
         copy.wait()
+    theta_out_ref[...] = theta_ref[...]
     theta = theta_ref[...].T
     diag = iota((chans, chans), 0) == iota((chans, chans), 1)
     amp = jnp.sum(jnp.where(diag, amp_ref[...], 0.0), axis=1, keepdims=True)
@@ -228,9 +231,9 @@
             lost.append(jnp.sum(jnp.where(r == c, two, 0.0), axis=0, keepdims=True))
         last = folds.pop()
         folds.append(jnp.concatenate([last[: chans // 2, :chans], last[chans // 2 :, :chans]], 1))
-        wide = jnp.broadcast_to(live_total, (1, 128))
-        folds.append(jnp.concatenate(lost + [wide, jnp.zeros((4, 128), F32)], 0))
-        folds.append(jnp.concatenate([grad, jnp.zeros((basis, 128 - chans), F32)], 1))
+        lost = [line[:, e * chans : (e + 1) * chans] for line in lost for e in range(2)][:5]
+        lost += [jnp.broadcast_to(live_total, (1, chans)), jnp.zeros((2, chans), F32)]
+        folds.append(jnp.concatenate([grad, jnp.concatenate(lost, 0)], 1))
         packs.append(folds)
     at = 0
     for one, two in zip(*packs):
@@ -240,7 +243,17 @@
         at += one.shape[0]
 
 
-def factor_block(tiles, base):
+def take(beside):
+    while beside:
+        try:
+            next(beside[0])
+            return True
+        except StopIteration:
+            beside.pop(0)
+    return False
+
+
+def factor_block(tiles, base, beside):
     count = len(tiles)
     tiles = list(tiles)
     sub = iota((8, 128), 0)
@@ -254,33 +267,44 @@
 
     ahead = {}
     for g in range(count):
-        here = range(g, count)
+        near = range(g, min(g + 1 + AHEAD, count))
+        far = range(near[-1] + 1, count)
         cols = {
             t: ahead[t] if t in ahead else [column(t, base + 8 * g + m) for m in range(8)]
-            for t in here
+            for t in range(g, count)
         }
-        ahead = {
-            t: [column(t, base + 8 * g + 8 + m) for m in range(8)]
-            for t in range(g + 1, min(g + 1 + AHEAD, count))
-        }
+        ahead = {t: [column(t, base + 8 * g + 8 + m) for m in range(8)] for t in near[1:]}
         kept = jnp.zeros((8, 128), F32)
+        solved = tiles[g]
         for m in range(8):
             inverse = 1.0 / spread(cols[g][m][m : m + 1])
             kept = jnp.where(sub == m, inverse, kept)
-            mult = {t: cols[t][m] * inverse for t in here}
+            own = cols[g][m]
+            for n in range(m + 1, 8):
+                scaled = spread(cols[g][n][m : m + 1]) * inverse
+                for t in near:
+                    cols[t][n] = cols[t][n] - cols[t][m] * scaled
+                if far:
+                    cols[g][n] = jnp.where(sub == m, scaled, cols[g][n])
+            mult = {t: cols[t][m] * inverse for t in near}
             mult[g] = jnp.where(sub > m, mult[g], 0.0)
-            for n in range(m + 1, 8):
-                pivot = spread(cols[g][n][m : m + 1])
-                for t in here:
-                    cols[t][n] = cols[t][n] - mult[t] * pivot
             for n in range(8 if ahead else 0):
                 pivot = spread(cols[g + 1][m][n : n + 1])
                 for t in ahead:
                     ahead[t][n] = ahead[t][n] - mult[t] * pivot
             pivot = spread(tiles[g][m : m + 1])
-            for t in here:
+            for t in near:
                 tiles[t] = tiles[t] - mult[t] * pivot
+            if far:
+                pivot = spread(solved[m : m + 1]) * inverse
+                solved = jnp.where(sub == m, pivot, solved - own * pivot)
+        for m in range(8 if far else 0):
+            pivot = spread(solved[m : m + 1])
+            for t in far:
+                tiles[t] = tiles[t] - cols[t][m] * pivot
         inverses.append(kept)
+        if g % PACE == 0:
+            beside()
     return tiles, inverses
 
 
@@ -313,7 +337,7 @@
     pack_ref[2 * half + (1 - quarter)] = q2_ref[...]
     pack_ref[2 * (1 - half) + (1 - quarter)] = q3_ref[...]
 
-    total = pack_ref[0, PACK - 13 : PACK - 12, :1]
+    total = pack_ref[0, PACK - 3 : PACK - 2, chans : chans + 1]
     scale = 1.0 / total
     r = iota((chans, chans), 0)
     c = iota((chans, chans), 1)
@@ -322,7 +346,7 @@
         plain_ref[k * chans : (k + 1) * chans, l * chans : (l + 1) * chans] = block
 
     for q in range(4):
-        lost = pack_ref[q, PACK - 16 : PACK - 13, :]
+        lost = pack_ref[q, PACK - 8 :, chans:]
         for i in range(2):
             fold = pack_ref[q, i * chans : (i + 1) * chans, :]
             turned = fold.T
@@ -330,7 +354,7 @@
             for e in range(2):
                 lane = slice(e * chans, (e + 1) * chans)
                 f, ft = fold[:, lane], turned[lane]
-                second = jnp.where(r == c, lost[i : i + 1, lane], jnp.where(r < c, f, ft))
+                second = jnp.where(r == c, lost[2 * i + e : 2 * i + e + 1], jnp.where(r < c, f, ft))
                 for d, block in ((i + e, jnp.where(r >= c, f, ft)), (i + e + 2, second)):
                     l = (k + d) % basis
                     put(k, l, block)
@@ -340,7 +364,7 @@
         f = jnp.concatenate([last[:, :chans], last[:, chans:]], 0)
         ft = f.T
         put(2 * q, (2 * q + basis // 2) % basis, jnp.where(r >= c, f, ft))
-        second = jnp.where(r == c, lost[2:, :chans], jnp.where(r < c, f, ft))
+        second = jnp.where(r == c, lost[4:5], jnp.where(r < c, f, ft))
         put(2 * q + 1, 2 * q + 1, second)
     tiles = params // 128
     per = 128 // chans
@@ -349,24 +373,35 @@
             mixed_ref[b, pl.ds(k, chans, stride=basis), :] = plain_ref[
                 k * chans : (k + 1) * chans, b * 128 : (b + 1) * 128
             ]
-    for a in range(tiles):
+    damping = damping_ref[0, 0]
+    spot = iota((128, 128), 0) == iota((128, 128), 1)
+
+    def fill(a):
+        rows = (a + 1) * 128 // basis
         for b in range(tiles):
             t = mixed_ref[b, a * 128 : (a + 1) * 128, :].T * scale
             for e in range(per):
-                n_ref[a, pl.ds(b * per + e, chans, stride=basis), :] = t[
-                    e * chans : (e + 1) * chans
+                n_ref[a, pl.ds(b * per + e, rows, stride=basis), :] = t[
+                    e * chans : e * chans + rows
                 ]
-    grad = (pack_ref[0, PACK - 8 :, :] * scale).T[:chans]
-    for k in range(basis):
-        n_ref[tiles, pl.ds(k, chans, stride=basis), :] = jnp.broadcast_to(
-            grad[:, k : k + 1], (chans, 128)
-        )
-
-    damping = damping_ref[0, 0]
-    for t in range(tiles):
-        at = slice(t * 128, (t + 1) * 128)
-        spot = iota((128, 128), 0) == iota((128, 128), 1)
-        n_ref[t, at, :] = n_ref[t, at, :] + jnp.where(spot, damping, 0.0)
+        at = slice(a * 128, (a + 1) * 128)
+        n_ref[a, at, :] = n_ref[a, at, :] + jnp.where(spot, damping, 0.0)
+
+    def fill_grad():
+        grad = (pack_ref[0, PACK - 8 :, :] * scale).T[:chans]
+        for k in range(basis):
+            n_ref[tiles, pl.ds(k, chans, stride=basis), :] = jnp.broadcast_to(
+                grad[:, k : k + 1], (chans, 128)
+            )
+
+    def fill_all():
+        for a in range(1, tiles):
+            fill(a)
+            yield
+        fill_grad()
+
+    fill(0)
+    beside = [fill_all()]
 
     lane = iota((BLK, 128), 1)
     sub = iota((BLK, 128), 0)
@@ -378,51 +413,103 @@
     def factor(block, base):
         eye = jnp.where(lane - (BLK - base) == sub, 1.0, 0.0)
         whole = jnp.where((lane >= base) & (lane < base + BLK), block, eye)
-        parts, inverses = factor_block([whole[8 * t : 8 * t + 8] for t in range(BLK // 8)], base)
+        parts = [whole[8 * t : 8 * t + 8] for t in range(BLK // 8)]
+        parts, inverses = factor_block(parts, base, lambda: take(beside) or take(spare))
         return jnp.concatenate([p * (i * lax.rsqrt(i)) for p, i in zip(parts, inverses)], 0)
 
+    def below(x):
+        return jnp.concatenate([jnp.zeros(x.shape, F32), x], 0)
+
+    def join(at, begin):
+        return jnp.concatenate([n_ref[t, at, :] for t in range(begin, tiles + 1)], 1)
+
+    def update(i, turned, part):
+        at = slice(i * 128, (i + 1) * 128)
+        change = mm(turned, part)
+        begin = tiles + 1 - part.shape[1] // 128
+        for t in range(begin, tiles + 1):
+            n_ref[t, at, :] = n_ref[t, at, :] - change[:, (t - begin) * 128 :][:, :128]
+
+    def early(j, top, low, inv0, cross, held):
+        if j + 1 < tiles:
+            held["near0"] = mm(inv0, below(n_ref[j + 1, top, :]))
+            yield
+            held["near_mid"] = n_ref[j + 1, low, :] - mm(cross, held["near0"])
+            at = slice((j + 1) * 128, (j + 2) * 128)
+            turned = held["near0"].T
+            yield
+            n_ref[j + 1, at, :] = n_ref[j + 1, at, :] - mm(turned, held["near0"])
+            yield
+        begin = min(j + 2, tiles)
+        held["rest0"] = mm(inv0, below(join(top, begin)))
+        yield
+        held["middle"] = join(low, begin) - mm(cross, held["rest0"])
+        yield
+
+    def late(j, inv1, near, held):
+        here = slice(j * 128, (j + 1) * 128)
+        rest1 = mm(inv1, held["middle"])
+        rest = jnp.concatenate([held["rest0"], rest1], 0)
+        held["rest"] = rest
+        if near is not None:
+            held["rest"] = jnp.concatenate([near, rest], 1)
+            turned = near.T
+            yield
+            update(j + 1, turned, rest)
+            yield
+            if j + 2 < tiles:
+                r_ref[here, (j + 2) * 128 :] = rest[:, :-128]
+            for i in range(j + 2, tiles):
+                part = rest[:, (i - j - 2) * 128 :]
+                update(i, part[:, :128].T, part)
+                yield
+
+    def solve(j, first, w0, w1, held):
+        rest = held["rest"]
+        turn1 = dot3(w1.T[:BLK], rest[BLK:])
+        up0 = w0.T[BLK:]
+        link = jnp.where(lane >= BLK, dot3(up0, first), 0.0)
+        yield
+        turn0 = dot3(up0, rest[:BLK]) - dot3(link, below(turn1))
+        turn = jnp.concatenate([turn0, turn1], 0)
+        for t in range(j + 1, tiles + 1):
+            t_ref[j, t] = turn[:, (t - j - 1) * 128 : (t - j) * 128]
+
+    spare = []
     for j in range(tiles):
         top = slice(j * 128, j * 128 + BLK)
         low = slice(j * 128 + BLK, (j + 1) * 128)
-        if j:
-            r_ref[j * 128 : (j + 1) * 128, : j * 128] = jnp.zeros((128, j * 128), F32)
+        here = slice(j * 128, (j + 1) * 128)
         w0 = factor(n_ref[j, top, :], 0)
         inv0 = jnp.where(lane >= BLK, w0, 0.0)
-        first = mm(inv0, jnp.concatenate([zeros, n_ref[j, top, :]], 0))
-        r_ref[top, j * 128 : (j + 1) * 128] = jnp.where(
-            lane >= BLK, first, jnp.where(lane >= sub, w0, 0.0)
-        )
+        first = mm(inv0, below(n_ref[j, top, :]))
         cross = first[:, BLK:].T
+        held = {}
+        beside.append(early(j, top, low, inv0, cross, held))
         w1 = factor(n_ref[j, low, :] - mm(cross, first), BLK)
-        r_ref[low, j * 128 : (j + 1) * 128] = jnp.where(lane - BLK >= sub, w1, 0.0)
+        while take(beside):
+            pass
         inv1 = w1[:, :BLK]
-        over0 = load(top, j + 1)
-        rest0 = mm(inv0, jnp.concatenate([jnp.zeros(over0.shape, F32), over0], 0))
-        rest1 = mm(inv1, load(low, j + 1) - mm(cross, rest0))
-        rest = jnp.concatenate([rest0, rest1], 0)
+        near = None
         if j + 1 < tiles:
-            r_ref[j * 128 : (j + 1) * 128, (j + 1) * 128 :] = rest[:, :-128]
-            for i in range(j + 1, tiles):
-                begin = (i - j - 1) * 128
-                turned = rest[:, begin : begin + 128].T
-                update = mm(turned, rest[:, begin:])
-                at = slice(i * 128, (i + 1) * 128)
-                for t in range(i, tiles + 1):
-                    n_ref[t, at, :] = n_ref[t, at, :] - update[:, (t - i) * 128 : (t - i + 1) * 128]
-        turn1 = mm(w1.T[:BLK], rest1)
-        whole0 = mm(w0.T[BLK:], jnp.concatenate([first, rest0], 1))
-        link = jnp.where(lane >= BLK, whole0[:, :128], 0.0)
-        turn0 = whole0[:, 128:] - mm(
-            link, jnp.concatenate([jnp.zeros(turn1.shape, F32), turn1], 0)
-        )
-        turn = jnp.concatenate([turn0, turn1], 0)
-        for t in range(j + 1, tiles + 1):
-            t_ref[j, t] = turn[:, (t - j - 1) * 128 : (t - j) * 128]
+            near1 = mm(inv1, held["near_mid"])
+            at = slice((j + 1) * 128, (j + 2) * 128)
+            n_ref[j + 1, at, :] = n_ref[j + 1, at, :] - mm(near1.T, near1)
+            near = jnp.concatenate([held["near0"], near1], 0)
+            r_ref[here, at] = near
+        if j:
+            r_ref[here, : j * 128] = jnp.zeros((128, j * 128), F32)
+        r_ref[top, here] = jnp.where(lane >= BLK, first, jnp.where(lane >= sub, w0, 0.0))
+        r_ref[low, here] = jnp.where(lane - BLK >= sub, w1, 0.0)
+        beside.append(late(j, inv1, near, held))
+        spare.append(solve(j, first, w0, w1, held))
+    while take(beside) or take(spare):
+        pass
 
     for j in reversed(range(tiles)):
         x = t_ref[j, tiles]
         if j + 1 < tiles:
-            x = x - mm(
+            x = x - dot3(
                 jnp.concatenate([t_ref[j, t] for t in range(j + 1, tiles)], 1),
                 x_ref[(j + 1) * 128 :, :],
             )
@@ -441,10 +528,6 @@
     pred_ref[...] = resid_ref[...] + jnp.sum(slope_ref[...] * weight, axis=0, keepdims=True)
 
 
-def flips(size, bit):
-    return [(i, i ^ bit) for i in range(size)]
-
-
 def on_device(images, gauge_pixel, row_mask, gauge_counts, targets, theta, amplitude, damping):
     nrows = lax.axis_size("rows")
     ncols = lax.axis_size("cols")
@@ -456,7 +539,7 @@
     pixel_rows = images.shape[0] * images.shape[1]
     theta_t = theta.T
     shape = jax.ShapeDtypeStruct
-    keep, send, slope, phi, resid = pl.pallas_call(
+    keep, send, slope, phi, resid, theta_here = pl.pallas_call(
         functools.partial(front, ncols),
         out_shape=[
             pltpu.VMEM((PACK, 128), F32),
@@ -464,9 +547,10 @@
             pltpu.VMEM((chans, share), F32),
             pltpu.VMEM((basis, share), F32),
             pltpu.VMEM((1, share), F32),
+            pltpu.VMEM((basis, chans), F32),
         ],
         in_specs=[SMEM] + [HBM] * 6,
-        out_specs=[VMEM] * 5,
+        out_specs=[VMEM] * 6,
         scratch_shapes=[
             pltpu.VMEM((pixel_rows, breadth), F32),
             pltpu.VMEM((1, slots), jnp.int32),
@@ -495,21 +579,28 @@
         amplitude.reshape(1, chans),
     )
 
-    bit = 1
+    def swap(x, row_bit, col_bit):
+        pairs = [
+            (r * ncols + c, (r ^ row_bit) * ncols + (c ^ col_bit))
+            for r in range(nrows)
+            for c in range(ncols)
+        ]
+        return lax.ppermute(x, ("rows", "cols"), pairs)
+
+    bits = [1 << i for i in range(nrows.bit_length() - 1)]
     if ncols == 2:
-        keep = keep + lax.ppermute(send, "rows", flips(nrows, 1))
-        bit = 2
-    while bit < nrows:
-        keep = keep + lax.ppermute(keep, "rows", flips(nrows, bit))
-        bit *= 2
-    if ncols == 2:
-        other_half = lax.ppermute(keep, "cols", flips(ncols, 1))
-        other_quarter = lax.ppermute(keep, "rows", flips(nrows, 1))
-        other_both = lax.ppermute(other_half, "rows", flips(nrows, 1))
+        core, across = (1, 0), 1
+        keep = keep + swap(send, *core)
+        bits = bits[1:]
     else:
-        other_half = lax.ppermute(keep, "cols", flips(ncols, 2))
-        other_quarter = lax.ppermute(keep, "cols", flips(ncols, 1))
-        other_both = lax.ppermute(other_half, "cols", flips(ncols, 1))
+        core, across = (0, 1), 2
+    last = bits.pop(max(len(bits) - 2, 0))
+    for bit in bits:
+        keep = keep + swap(keep, bit, 0)
+    same, other, both = swap(keep, last, 0), swap(keep, 0, across), swap(keep, last, across)
+    keep, other_half = keep + same, other + both
+    other_quarter = swap(keep, *core)
+    other_both = swap(other_half, *core)
 
     r_factor, new_theta, predicted = pl.pallas_call(
         functools.partial(back, ncols),
@@ -539,7 +630,7 @@
         slope,
         phi,
         resid,
-        theta_t,
+        theta_here,
     )
     return r_factor, new_theta.T, predicted.reshape(share)
 

time: 49.4 us -> 47.7 us (0.966)
  waiting for transfers between devices: 12.6 us -> 11 us
    ppermute x7 -> x8, waiting for transfers between devices: 12.6 us -> 11 us  [swap(): return lax.ppermute(x, ('rows', 'cols'), pairs)]
    ppermute x7 -> x8, starting transfers between devices: 10 us -> 10.4 us  [swap(): return lax.ppermute(x, ('rows', 'cols'), pairs)]
  transfers between devices with their start and end apart: 7 -> 8, of which waited for: 6 -> 7; matrix products, arithmetic and copies ran while one was open for 0% -> 0% of each run, Pallas kernels for 0% -> 0%
where the time goes in v2:
time: 47.7 us; the launch traced here: 47.5 us
  Pallas kernels  24.1 us (51%)
  waiting for transfers between devices  11 us (23%)
  starting transfers between devices  10.4 us (22%)
  between operations  1.96 us (4%)
    pallas_call x1, Pallas kernels, on_device(): pl.pallas_call(functools.partial(back, ncols), out_shape=[shape((params,...  16.2 us
    ppermute x8, waiting for transfers between devices, swap(): return lax.ppermute(x, ('rows', 'cols'), pairs)  11 us
    ppermute x8, starting transfers between devices, swap(): return lax.ppermute(x, ('rows', 'cols'), pairs)  10.4 us
    pallas_call x1, Pallas kernels, on_device(): pl.pallas_call(functools.partial(front, ncols), out_shape=[pltpu.VMEM((PA...  7.87 us
  transfers between devices with their start and end apart: 8, of which 7 were waited for; matrix products, arithmetic and copies ran while one was open for 0% of the time, Pallas kernels for 0%

profile of v2, /device:TPU:0, one launch (start us, length us, event | category | flops | bytes accessed | tf_op | source)
XLA Modules:
  0.0 47.5 jit_solution(3675096788853151765)
XLA Ops:
  1.3 7.9 %front.1 = (f32[168,128]{1,0:T(8,128)S(1)}, f32[168,128]{1,0:T(8,128)S(1)}, f32[64,1024]{1,0:T(8,128)S(1)}, f32[8,1024]{1,0:T(8,128)S(1)}, f32[1,1024]{1,0:T(1,128)S(1)}, /*index=5*/f32[8,64]{1,0:T(8,128)S(1)}) custom-call(s32[1]{0:T(128)S(6)} %copy.11.count_ref, f32[256,128]{1,0:T(8,128)} %bitcast.10, s32[1,2048]{1,0:T(1,128)} %bitcast.11, ...), custom_call_target="tpu_custom_call" | custom-call | tf_op jit(solution)/shard_map/front/pallas_call | solution.py:542
  9.2 0.5 %collective-permute-start = (f32[168,128]{1,0:T(8,128)S(1)}, f32[168,128]{1,0:T(8,128)S(1)}, u32[]{:S(2)}, u32[]{:S(2)}) collective-permute-start(f32[168,128]{1,0:T(8,128)S(1)} %get-tuple-element.13), channel_id=1, source_target_pairs={{0,2},{1,3},{2,0},{3,1},{4,6},{5,7},{6,4},{7,5},{8,10},{9,11},{10,... | collective-permute-start | bytes 258056 | tf_op jit(solution)/shard_map/ppermute | solution.py:588
  9.7 0.9 %collective-permute-done = f32[168,128]{1,0:T(8,128)S(1)} collective-permute-done((f32[168,128]{1,0:T(8,128)S(1)}, f32[168,128]{1,0:T(8,128)S(1)}, u32[]{:S(2)}, u32[]{:S(2)}) %collective-permute-start) | collective-permute-done | bytes 86048 | tf_op jit(solution)/shard_map/ppermute | solution.py:588
  10.6 2.9 %collective-permute-start.1 = (f32[168,128]{1,0:T(8,128)S(1)}, f32[168,128]{1,0:T(8,128)S(1)}, u32[]{:S(2)}, u32[]{:S(2)}) collective-permute-start(f32[168,128]{1,0:T(8,128)S(1)} %add.15), channel_id=1, source_target_pairs={{0,4},{1,5},{2,6},{3,7},{4,0},{5,1},{6,2},{7,3},{8,12},{9,13},{10,... | collective-permute-start | bytes 258056 | tf_op jit(solution)/shard_map/ppermute | solution.py:588
  13.6 2.9 %collective-permute-done.1 = f32[168,128]{1,0:T(8,128)S(1)} collective-permute-done((f32[168,128]{1,0:T(8,128)S(1)}, f32[168,128]{1,0:T(8,128)S(1)}, u32[]{:S(2)}, u32[]{:S(2)}) %collective-permute-start.1) | collective-permute-done | bytes 86048 | tf_op jit(solution)/shard_map/ppermute | solution.py:588
  16.4 2.9 %collective-permute-start.2 = (f32[168,128]{1,0:T(8,128)S(1)}, f32[168,128]{1,0:T(8,128)S(1)}, u32[]{:S(2)}, u32[]{:S(2)}) collective-permute-start(f32[168,128]{1,0:T(8,128)S(1)} %add.16), channel_id=1, source_target_pairs={{0,16},{1,17},{2,18},{3,19},{4,20},{5,21},{6,22},{7,23},{8,24},{9,... | collective-permute-start | bytes 258056 | tf_op jit(solution)/shard_map/ppermute | solution.py:588
  19.3 4.0 %collective-permute-done.2 = f32[168,128]{1,0:T(8,128)S(1)} collective-permute-done((f32[168,128]{1,0:T(8,128)S(1)}, f32[168,128]{1,0:T(8,128)S(1)}, u32[]{:S(2)}, u32[]{:S(2)}) %collective-permute-start.2) | collective-permute-done | bytes 86048 | tf_op jit(solution)/shard_map/ppermute | solution.py:588
  23.3 1.6 %collective-permute-start.5 = (f32[168,128]{1,0:T(8,128)S(1)}, f32[168,128]{1,0:T(8,128)S(1)}, u32[]{:S(2)}, u32[]{:S(2)}) collective-permute-start(f32[168,128]{1,0:T(8,128)S(1)} %add.17), channel_id=1, source_target_pairs={{0,9},{1,8},{2,11},{3,10},{4,13},{5,12},{6,15},{7,14},{8,1},{9,0},... | collective-permute-start | bytes 258056 | tf_op jit(solution)/shard_map/ppermute | solution.py:588
  24.9 0.5 %collective-permute-start.4 = (f32[168,128]{1,0:T(8,128)S(1)}, f32[168,128]{1,0:T(8,128)S(1)}, u32[]{:S(2)}, u32[]{:S(2)}) collective-permute-start(f32[168,128]{1,0:T(8,128)S(1)} %add.17), channel_id=1, source_target_pairs={{0,1},{1,0},{2,3},{3,2},{4,5},{5,4},{6,7},{7,6},{8,9},{9,8},{10,11... | collective-permute-start | bytes 258056 | tf_op jit(solution)/shard_map/ppermute | solution.py:588
  25.4 1.5 %collective-permute-start.3 = (f32[168,128]{1,0:T(8,128)S(1)}, f32[168,128]{1,0:T(8,128)S(1)}, u32[]{:S(2)}, u32[]{:S(2)}) collective-permute-start(f32[168,128]{1,0:T(8,128)S(1)} %add.17), channel_id=1, source_target_pairs={{0,8},{1,9},{2,10},{3,11},{4,12},{5,13},{6,14},{7,15},{8,0},{9,1},... | collective-permute-start | bytes 258056 | tf_op jit(solution)/shard_map/ppermute | solution.py:588
  26.9 1.9 %collective-permute-done.5 = f32[168,128]{1,0:T(8,128)S(1)} collective-permute-done((f32[168,128]{1,0:T(8,128)S(1)}, f32[168,128]{1,0:T(8,128)S(1)}, u32[]{:S(2)}, u32[]{:S(2)}) %collective-permute-start.5) | collective-permute-done | bytes 86048 | tf_op jit(solution)/shard_map/ppermute | solution.py:588
  28.8 0.9 %collective-permute-done.4 = f32[168,128]{1,0:T(8,128)S(1)} collective-permute-done((f32[168,128]{1,0:T(8,128)S(1)}, f32[168,128]{1,0:T(8,128)S(1)}, u32[]{:S(2)}, u32[]{:S(2)}) %collective-permute-start.4) | collective-permute-done | bytes 86048 | tf_op jit(solution)/shard_map/ppermute | solution.py:588
  29.7 0.1 collective-permute-start.7
  29.8 0.1 collective-permute-done.3
  29.9 0.5 collective-permute-start.6
  31.0 0.0 collective-permute-done.7.q3_ref
  31.1 0.2 collective-permute-done.6.q2_ref
  31.3 16.2 %back.1 = (f32[512,512]{1,0:T(8,128)}, f32[8,64]{1,0:T(8,128)}, f32[1,1024]{1,0:T(1,128)}) custom-call(f32[1,1]{1,0:T(1,128)} %bitcast.9.damping_ref, f32[168,128]{1,0:T(8,128)S(1)} %add.18.q0_ref, f32[168,128]{1,0:T(8,128)S(1)} %add.19.q1_ref, f32[168,128]{1,0:T(8,128)S(1)} %collective-permute-done.6.q2_ref, f32[168,128]{1,0:T(8,128)S(1)} %collective-permute-done.7.q3_ref, ...), custom_call_target="tpu_custom_call" | custom-call | tf_op jit(solution)/shard_map/back/pallas_call | solution.py:605
  (5 shorter events, 0.1 us)
Async XLA Ops:
  9.2 1.4 %collective-permute-start = (f32[168,128]{1,0:T(8,128)S(1)}, f32[168,128]{1,0:T(8,128)S(1)}, u32[]{:S(2)}, u32[]{:S(2)}) collective-permute-start(f32[168,128]{1,0:T(8,128)S(1)} %get-tuple-element.13), channel_id=1, source_target_pairs={{0,2},{1,3},{2,0},{3,1},{4,6},{5,7},{6,4},{7,5},{8,10},{9,11},{10,... | collective-permute-start | bytes 258056 | tf_op jit(solution)/shard_map/ppermute | solution.py:588
  10.6 5.8 %collective-permute-start.1 = (f32[168,128]{1,0:T(8,128)S(1)}, f32[168,128]{1,0:T(8,128)S(1)}, u32[]{:S(2)}, u32[]{:S(2)}) collective-permute-start(f32[168,128]{1,0:T(8,128)S(1)} %add.15), channel_id=1, source_target_pairs={{0,4},{1,5},{2,6},{3,7},{4,0},{5,1},{6,2},{7,3},{8,12},{9,13},{10,... | collective-permute-start | bytes 258056 | tf_op jit(solution)/shard_map/ppermute | solution.py:588
  16.4 6.9 %collective-permute-start.2 = (f32[168,128]{1,0:T(8,128)S(1)}, f32[168,128]{1,0:T(8,128)S(1)}, u32[]{:S(2)}, u32[]{:S(2)}) collective-permute-start(f32[168,128]{1,0:T(8,128)S(1)} %add.16), channel_id=1, source_target_pairs={{0,16},{1,17},{2,18},{3,19},{4,20},{5,21},{6,22},{7,23},{8,24},{9,... | collective-permute-start | bytes 258056 | tf_op jit(solution)/shard_map/ppermute | solution.py:588
  23.3 5.5 %collective-permute-start.5 = (f32[168,128]{1,0:T(8,128)S(1)}, f32[168,128]{1,0:T(8,128)S(1)}, u32[]{:S(2)}, u32[]{:S(2)}) collective-permute-start(f32[168,128]{1,0:T(8,128)S(1)} %add.17), channel_id=1, source_target_pairs={{0,9},{1,8},{2,11},{3,10},{4,13},{5,12},{6,15},{7,14},{8,1},{9,0},... | collective-permute-start | bytes 258056 | tf_op jit(solution)/shard_map/ppermute | solution.py:588
  24.9 4.8 %collective-permute-start.4 = (f32[168,128]{1,0:T(8,128)S(1)}, f32[168,128]{1,0:T(8,128)S(1)}, u32[]{:S(2)}, u32[]{:S(2)}) collective-permute-start(f32[168,128]{1,0:T(8,128)S(1)} %add.17), channel_id=1, source_target_pairs={{0,1},{1,0},{2,3},{3,2},{4,5},{5,4},{6,7},{7,6},{8,9},{9,8},{10,11... | collective-permute-start | bytes 258056 | tf_op jit(solution)/shard_map/ppermute | solution.py:588
  25.4 4.5 %collective-permute-start.3 = (f32[168,128]{1,0:T(8,128)S(1)}, f32[168,128]{1,0:T(8,128)S(1)}, u32[]{:S(2)}, u32[]{:S(2)}) collective-permute-start(f32[168,128]{1,0:T(8,128)S(1)} %add.17), channel_id=1, source_target_pairs={{0,8},{1,9},{2,10},{3,11},{4,12},{5,13},{6,14},{7,15},{8,0},{9,1},... | collective-permute-start | bytes 258056 | tf_op jit(solution)/shard_map/ppermute | solution.py:588
  29.7 1.3 %collective-permute-start.7 = (f32[168,128]{1,0:T(8,128)S(1)}, f32[168,128]{1,0:T(8,128)S(1)}, u32[]{:S(2)}, u32[]{:S(2)}) collective-permute-start(f32[168,128]{1,0:T(8,128)S(1)} %add.19.q1_ref), channel_id=1, source_target_pairs={{0,2},{1,3},{2,0},{3,1},{4,6},{5,7},{6,4},{7,5},{8,10},{9,11},{10,... | collective-permute-start | bytes 258056 | tf_op jit(solution)/shard_map/ppermute | solution.py:588
  29.9 1.4 %collective-permute-start.6 = (f32[168,128]{1,0:T(8,128)S(1)}, f32[168,128]{1,0:T(8,128)S(1)}, u32[]{:S(2)}, u32[]{:S(2)}) collective-permute-start(f32[168,128]{1,0:T(8,128)S(1)} %add.18.q0_ref), channel_id=1, source_target_pairs={{0,2},{1,3},{2,0},{3,1},{4,6},{5,7},{6,4},{7,5},{8,10},{9,11},{10,... | collective-permute-start | bytes 258056 | tf_op jit(solution)/shard_map/ppermute | solution.py:588

commit v3 on v2

--- a/solution.py
+++ b/solution.py
@@ -20,7 +20,7 @@
 HBM = pl.BlockSpec(memory_space=pltpu.HBM)
 SMEM = pl.BlockSpec(memory_space=pltpu.SMEM)
 PACK = 168
-CHUNK = 512
+CHUNK = 256
 PACE = 1
 AHEAD = 2
 BLK = 64

time: 47.7 us -> 47.6 us (level)
  no operation moved by 1% of the time
where the time goes in v3:
time: 47.6 us; the launch traced here: 47.4 us
  Pallas kernels  24 us (50%)
  waiting for transfers between devices  11 us (23%)
  starting transfers between devices  10.4 us (22%)
  between operations  1.96 us (4%)
    pallas_call x1, Pallas kernels, on_device(): pl.pallas_call(functools.partial(back, ncols), out_shape=[shape((params,...  16.2 us
    ppermute x8, waiting for transfers between devices, swap(): return lax.ppermute(x, ('rows', 'cols'), pairs)  11 us
    ppermute x8, starting transfers between devices, swap(): return lax.ppermute(x, ('rows', 'cols'), pairs)  10.4 us
    pallas_call x1, Pallas kernels, on_device(): pl.pallas_call(functools.partial(front, ncols), out_shape=[pltpu.VMEM((PA...  7.72 us
  transfers between devices with their start and end apart: 8, of which 7 were waited for; matrix products, arithmetic and copies ran while one was open for 0% of the time, Pallas kernels for 0%

profile of v3, /device:TPU:0, one launch (start us, length us, event | category | flops | bytes accessed | tf_op | source)
XLA Modules:
  0.0 47.4 jit_solution(13029578984576716066)
XLA Ops:
  1.3 7.7 %front.1 = (f32[168,128]{1,0:T(8,128)S(1)}, f32[168,128]{1,0:T(8,128)S(1)}, f32[64,1024]{1,0:T(8,128)S(1)}, f32[8,1024]{1,0:T(8,128)S(1)}, f32[1,1024]{1,0:T(1,128)S(1)}, /*index=5*/f32[8,64]{1,0:T(8,128)S(1)}) custom-call(s32[1]{0:T(128)S(6)} %copy.11.count_ref, f32[256,128]{1,0:T(8,128)} %bitcast.10, s32[1,2048]{1,0:T(1,128)} %bitcast.11, ...), custom_call_target="tpu_custom_call" | custom-call | tf_op jit(solution)/shard_map/front/pallas_call | solution.py:542
  9.0 0.5 %collective-permute-start = (f32[168,128]{1,0:T(8,128)S(1)}, f32[168,128]{1,0:T(8,128)S(1)}, u32[]{:S(2)}, u32[]{:S(2)}) collective-permute-start(f32[168,128]{1,0:T(8,128)S(1)} %get-tuple-element.13), channel_id=1, source_target_pairs={{0,2},{1,3},{2,0},{3,1},{4,6},{5,7},{6,4},{7,5},{8,10},{9,11},{10,... | collective-permute-start | bytes 258056 | tf_op jit(solution)/shard_map/ppermute | solution.py:588
  9.5 0.9 %collective-permute-done = f32[168,128]{1,0:T(8,128)S(1)} collective-permute-done((f32[168,128]{1,0:T(8,128)S(1)}, f32[168,128]{1,0:T(8,128)S(1)}, u32[]{:S(2)}, u32[]{:S(2)}) %collective-permute-start) | collective-permute-done | bytes 86048 | tf_op jit(solution)/shard_map/ppermute | solution.py:588
  10.5 2.9 %collective-permute-start.1 = (f32[168,128]{1,0:T(8,128)S(1)}, f32[168,128]{1,0:T(8,128)S(1)}, u32[]{:S(2)}, u32[]{:S(2)}) collective-permute-start(f32[168,128]{1,0:T(8,128)S(1)} %add.15), channel_id=1, source_target_pairs={{0,4},{1,5},{2,6},{3,7},{4,0},{5,1},{6,2},{7,3},{8,12},{9,13},{10,... | collective-permute-start | bytes 258056 | tf_op jit(solution)/shard_map/ppermute | solution.py:588
  13.4 2.9 %collective-permute-done.1 = f32[168,128]{1,0:T(8,128)S(1)} collective-permute-done((f32[168,128]{1,0:T(8,128)S(1)}, f32[168,128]{1,0:T(8,128)S(1)}, u32[]{:S(2)}, u32[]{:S(2)}) %collective-permute-start.1) | collective-permute-done | bytes 86048 | tf_op jit(solution)/shard_map/ppermute | solution.py:588
  16.3 2.9 %collective-permute-start.2 = (f32[168,128]{1,0:T(8,128)S(1)}, f32[168,128]{1,0:T(8,128)S(1)}, u32[]{:S(2)}, u32[]{:S(2)}) collective-permute-start(f32[168,128]{1,0:T(8,128)S(1)} %add.16), channel_id=1, source_target_pairs={{0,16},{1,17},{2,18},{3,19},{4,20},{5,21},{6,22},{7,23},{8,24},{9,... | collective-permute-start | bytes 258056 | tf_op jit(solution)/shard_map/ppermute | solution.py:588
  19.1 4.0 %collective-permute-done.2 = f32[168,128]{1,0:T(8,128)S(1)} collective-permute-done((f32[168,128]{1,0:T(8,128)S(1)}, f32[168,128]{1,0:T(8,128)S(1)}, u32[]{:S(2)}, u32[]{:S(2)}) %collective-permute-start.2) | collective-permute-done | bytes 86048 | tf_op jit(solution)/shard_map/ppermute | solution.py:588
  23.2 1.6 %collective-permute-start.5 = (f32[168,128]{1,0:T(8,128)S(1)}, f32[168,128]{1,0:T(8,128)S(1)}, u32[]{:S(2)}, u32[]{:S(2)}) collective-permute-start(f32[168,128]{1,0:T(8,128)S(1)} %add.17), channel_id=1, source_target_pairs={{0,9},{1,8},{2,11},{3,10},{4,13},{5,12},{6,15},{7,14},{8,1},{9,0},... | collective-permute-start | bytes 258056 | tf_op jit(solution)/shard_map/ppermute | solution.py:588
  24.8 0.5 %collective-permute-start.4 = (f32[168,128]{1,0:T(8,128)S(1)}, f32[168,128]{1,0:T(8,128)S(1)}, u32[]{:S(2)}, u32[]{:S(2)}) collective-permute-start(f32[168,128]{1,0:T(8,128)S(1)} %add.17), channel_id=1, source_target_pairs={{0,1},{1,0},{2,3},{3,2},{4,5},{5,4},{6,7},{7,6},{8,9},{9,8},{10,11... | collective-permute-start | bytes 258056 | tf_op jit(solution)/shard_map/ppermute | solution.py:588
  25.3 1.4 %collective-permute-start.3 = (f32[168,128]{1,0:T(8,128)S(1)}, f32[168,128]{1,0:T(8,128)S(1)}, u32[]{:S(2)}, u32[]{:S(2)}) collective-permute-start(f32[168,128]{1,0:T(8,128)S(1)} %add.17), channel_id=1, source_target_pairs={{0,8},{1,9},{2,10},{3,11},{4,12},{5,13},{6,14},{7,15},{8,0},{9,1},... | collective-permute-start | bytes 258056 | tf_op jit(solution)/shard_map/ppermute | solution.py:588
  26.7 1.9 %collective-permute-done.5 = f32[168,128]{1,0:T(8,128)S(1)} collective-permute-done((f32[168,128]{1,0:T(8,128)S(1)}, f32[168,128]{1,0:T(8,128)S(1)}, u32[]{:S(2)}, u32[]{:S(2)}) %collective-permute-start.5) | collective-permute-done | bytes 86048 | tf_op jit(solution)/shard_map/ppermute | solution.py:588
  28.6 0.9 %collective-permute-done.4 = f32[168,128]{1,0:T(8,128)S(1)} collective-permute-done((f32[168,128]{1,0:T(8,128)S(1)}, f32[168,128]{1,0:T(8,128)S(1)}, u32[]{:S(2)}, u32[]{:S(2)}) %collective-permute-start.4) | collective-permute-done | bytes 86048 | tf_op jit(solution)/shard_map/ppermute | solution.py:588
  29.6 0.1 collective-permute-start.7
  29.6 0.1 collective-permute-done.3
  29.8 0.4 collective-permute-start.6
  30.9 0.0 collective-permute-done.7.q3_ref
  30.9 0.2 collective-permute-done.6.q2_ref
  31.1 16.2 %back.1 = (f32[512,512]{1,0:T(8,128)}, f32[8,64]{1,0:T(8,128)}, f32[1,1024]{1,0:T(1,128)}) custom-call(f32[1,1]{1,0:T(1,128)} %bitcast.9.damping_ref, f32[168,128]{1,0:T(8,128)S(1)} %add.18.q0_ref, f32[168,128]{1,0:T(8,128)S(1)} %add.19.q1_ref, f32[168,128]{1,0:T(8,128)S(1)} %collective-permute-done.6.q2_ref, f32[168,128]{1,0:T(8,128)S(1)} %collective-permute-done.7.q3_ref, ...), custom_call_target="tpu_custom_call" | custom-call | tf_op jit(solution)/shard_map/back/pallas_call | solution.py:605
  (5 shorter events, 0.1 us)
Async XLA Ops:
  9.0 1.5 %collective-permute-start = (f32[168,128]{1,0:T(8,128)S(1)}, f32[168,128]{1,0:T(8,128)S(1)}, u32[]{:S(2)}, u32[]{:S(2)}) collective-permute-start(f32[168,128]{1,0:T(8,128)S(1)} %get-tuple-element.13), channel_id=1, source_target_pairs={{0,2},{1,3},{2,0},{3,1},{4,6},{5,7},{6,4},{7,5},{8,10},{9,11},{10,... | collective-permute-start | bytes 258056 | tf_op jit(solution)/shard_map/ppermute | solution.py:588
  10.5 5.8 %collective-permute-start.1 = (f32[168,128]{1,0:T(8,128)S(1)}, f32[168,128]{1,0:T(8,128)S(1)}, u32[]{:S(2)}, u32[]{:S(2)}) collective-permute-start(f32[168,128]{1,0:T(8,128)S(1)} %add.15), channel_id=1, source_target_pairs={{0,4},{1,5},{2,6},{3,7},{4,0},{5,1},{6,2},{7,3},{8,12},{9,13},{10,... | collective-permute-start | bytes 258056 | tf_op jit(solution)/shard_map/ppermute | solution.py:588
  16.3 6.9 %collective-permute-start.2 = (f32[168,128]{1,0:T(8,128)S(1)}, f32[168,128]{1,0:T(8,128)S(1)}, u32[]{:S(2)}, u32[]{:S(2)}) collective-permute-start(f32[168,128]{1,0:T(8,128)S(1)} %add.16), channel_id=1, source_target_pairs={{0,16},{1,17},{2,18},{3,19},{4,20},{5,21},{6,22},{7,23},{8,24},{9,... | collective-permute-start | bytes 258056 | tf_op jit(solution)/shard_map/ppermute | solution.py:588
  23.2 5.5 %collective-permute-start.5 = (f32[168,128]{1,0:T(8,128)S(1)}, f32[168,128]{1,0:T(8,128)S(1)}, u32[]{:S(2)}, u32[]{:S(2)}) collective-permute-start(f32[168,128]{1,0:T(8,128)S(1)} %add.17), channel_id=1, source_target_pairs={{0,9},{1,8},{2,11},{3,10},{4,13},{5,12},{6,15},{7,14},{8,1},{9,0},... | collective-permute-start | bytes 258056 | tf_op jit(solution)/shard_map/ppermute | solution.py:588
  24.8 4.8 %collective-permute-start.4 = (f32[168,128]{1,0:T(8,128)S(1)}, f32[168,128]{1,0:T(8,128)S(1)}, u32[]{:S(2)}, u32[]{:S(2)}) collective-permute-start(f32[168,128]{1,0:T(8,128)S(1)} %add.17), channel_id=1, source_target_pairs={{0,1},{1,0},{2,3},{3,2},{4,5},{5,4},{6,7},{7,6},{8,9},{9,8},{10,11... | collective-permute-start | bytes 258056 | tf_op jit(solution)/shard_map/ppermute | solution.py:588
  25.3 4.5 %collective-permute-start.3 = (f32[168,128]{1,0:T(8,128)S(1)}, f32[168,128]{1,0:T(8,128)S(1)}, u32[]{:S(2)}, u32[]{:S(2)}) collective-permute-start(f32[168,128]{1,0:T(8,128)S(1)} %add.17), channel_id=1, source_target_pairs={{0,8},{1,9},{2,10},{3,11},{4,12},{5,13},{6,14},{7,15},{8,0},{9,1},... | collective-permute-start | bytes 258056 | tf_op jit(solution)/shard_map/ppermute | solution.py:588
  29.6 1.3 %collective-permute-start.7 = (f32[168,128]{1,0:T(8,128)S(1)}, f32[168,128]{1,0:T(8,128)S(1)}, u32[]{:S(2)}, u32[]{:S(2)}) collective-permute-start(f32[168,128]{1,0:T(8,128)S(1)} %add.19.q1_ref), channel_id=1, source_target_pairs={{0,2},{1,3},{2,0},{3,1},{4,6},{5,7},{6,4},{7,5},{8,10},{9,11},{10,... | collective-permute-start | bytes 258056 | tf_op jit(solution)/shard_map/ppermute | solution.py:588
  29.8 1.4 %collective-permute-start.6 = (f32[168,128]{1,0:T(8,128)S(1)}, f32[168,128]{1,0:T(8,128)S(1)}, u32[]{:S(2)}, u32[]{:S(2)}) collective-permute-start(f32[168,128]{1,0:T(8,128)S(1)} %add.18.q0_ref), channel_id=1, source_target_pairs={{0,2},{1,3},{2,0},{3,1},{4,6},{5,7},{6,4},{7,5},{8,10},{9,11},{10,... | collective-permute-start | bytes 258056 | tf_op jit(solution)/shard_map/ppermute | solution.py:588
